TPU v7x, 256 devices: a whole 4x4x8 slice. The times are simulated.
256 devices in a mesh: grp: 16 (over z, core), sp: 16 (over x, y).
Axes of the slice: x: 4, y: 4, z: 8, core: 2. Of those that a mesh axis runs over, the one named last changes fastest.
Arguments:
- query: bfloat16 [32768, 4096], P(('grp', 'sp')), may hold values from -6 to 6
- key_value: bfloat16 [2, 32768, 512], P(None, ('grp', 'sp')), may hold values from -6 to 6
- grad_out: bfloat16 [32768, 4096], P(('grp', 'sp')), may hold values from -6 to 6
- segment_ids: int32 [16, 1, 2048], P('grp'), may hold values from 0 to 15, never falling along the last dimension, each value on 1 to 256 neighbouring positions
- lag: int32 [16, 1, 16], P('grp'), may hold values from 0 to 8
- q_gain: float32 [128], replicated, may hold values from 0.25 to 1.75
- k_gain: float32 [128], replicated, may hold values from 0.25 to 1.75
Outputs:
- attn_out: bfloat16 [32768, 4096], P(('grp', 'sp'))
- d_query: bfloat16 [32768, 4096], P(('grp', 'sp'))
- d_key_value: bfloat16 [2, 32768, 512], P(None, ('grp', 'sp'))
- d_q_gain: float32 [128], replicated
- d_k_gain: float32 [128], replicated
Inputs may be any that keep to these rules, and one draw needn't show every extreme that they name: `segment_ids`: segment ids never fall along a sequence; every response of 0 to 15 has 1 to 256 tokens in each sequence, one exactly 256.
All inputs are finite; a program needn't handle non-finite values.
Results may differ from a plain program's by a relative error of at most 0.019.
Values may be sent and summed in bfloat16 or wider, within the bound.
No kernel may reach another device: no remote copies, remote signals or barrier semaphores. Data moves between devices by JAX's collectives and lax.ppermute only.
A program may use at most 128 MiB of HBM per device.

v0:
```python
import jax
import jax.numpy as jnp
from jax import lax
from jax.sharding import PartitionSpec as P

EPS = 1e-06


def rms_parts(x):
    inverse_root_scale = lax.rsqrt(jnp.mean(x * x, -1, keepdims=True) + EPS)
    return (x * inverse_root_scale, inverse_root_scale)


def norm_backward_pass(upstream_gradient, normalized_input, inverse_root_scale, norm_weight):
    scaled_input = upstream_gradient * norm_weight
    return inverse_root_scale * (
        scaled_input
        - normalized_input * jnp.mean(scaled_input * normalized_input, -1, keepdims=True)
    )


def local(query, key_value, grad_out, segment_ids, lag, q_gain, k_gain):
    tok = query.shape[0]
    shards = lax.axis_size("sp")
    width = q_gain.shape[0]
    kv_heads = key_value.shape[2] // width
    q_heads = query.shape[1] // width
    per_dev = q_heads // shards
    seq = tok * shards
    length = segment_ids.shape[2]
    responses = lag.shape[2]
    scale = width ** (-0.5)
    rank = lax.axis_index("sp")
    segs = segment_ids[0]
    onehot = (segs[:, :, None] == jnp.arange(responses, dtype=jnp.int32)[None, None, :]).astype(
        jnp.float32
    )
    coef = 8.0 / (8.0 + lag[0].astype(jnp.float32))
    coef_all = jnp.sum(onehot * coef[:, None, :], 2).reshape(seq)
    token_coef = lax.dynamic_slice_in_dim(coef_all, rank * tok, tok)
    qhat, qrstd = rms_parts(query.astype(jnp.float32).reshape(tok, q_heads, width))
    khat, krstd = rms_parts(key_value[0].astype(jnp.float32).reshape(tok, kv_heads, width))
    qnormed = (qhat * q_gain).astype(jnp.bfloat16).reshape(tok, q_heads * width)
    knormed = (khat * k_gain).astype(jnp.bfloat16)
    scaled_grad = (grad_out.astype(jnp.float32) * token_coef[:, None]).astype(jnp.bfloat16)
    stacked = jnp.stack([qnormed, scaled_grad]).reshape(2, tok, shards, per_dev * width)
    moved = lax.all_to_all(stacked, "sp", split_axis=2, concat_axis=1, tiled=True).reshape(
        2, seq, per_dev, width
    )
    own_head = rank * kv_heads // shards
    pair = jnp.stack([knormed.reshape(tok, kv_heads * width), key_value[1]])
    full = lax.all_gather(pair, "sp", axis=1, tiled=True)
    own = lax.dynamic_slice_in_dim(full, own_head * width, width, 2)
    q_side = moved[0]
    g_side = moved[1]
    keys = own[0]
    vals = own[1]
    number = max(1, min(8, length // 512))
    while length % number:
        number = number - 1
    block = length // number
    positions = jnp.arange(length, dtype=jnp.int32)
    outs = []
    dqs = []
    seg_row = segs[0]
    dkey = jnp.zeros((length, width), jnp.float32)
    dval = jnp.zeros((length, width), jnp.float32)
    for index in range(number):
        lower = index * block
        upper = lower + block
        qblock = q_side[lower:upper]
        gblock = g_side[lower:upper]
        kpart = keys[0:upper]
        vpart = vals[0:upper]
        scores = (
            jnp.einsum("qhd,kd->hqk", qblock, kpart, preferred_element_type=jnp.float32) * scale
        )
        allowed = (positions[None, :upper] <= positions[lower:upper, None]) & (
            seg_row[None, :upper] == seg_row[lower:upper, None]
        )
        scores = jnp.where(allowed[None], scores, -jnp.inf)
        prob = jax.nn.softmax(scores, -1)
        pround = prob.astype(jnp.bfloat16)
        outb = jnp.einsum("hqk,kd->qhd", pround, vpart, preferred_element_type=jnp.float32).astype(
            jnp.bfloat16
        )
        delta = jnp.sum(gblock.astype(jnp.float32) * outb.astype(jnp.float32), -1)
        dprob = jnp.einsum("qhd,kd->hqk", gblock, vpart, preferred_element_type=jnp.float32)
        dsb = (prob * (dprob - delta.T[:, :, None]) * scale).astype(jnp.bfloat16)
        dqs.append(
            jnp.einsum("hqk,kd->qhd", dsb, kpart, preferred_element_type=jnp.float32).astype(
                jnp.bfloat16
            )
        )
        outs.append(outb)
        dkey = dkey.at[:upper].add(
            jnp.einsum("hqk,qhd->kd", dsb, qblock, preferred_element_type=jnp.float32)
        )
        dval = dval.at[:upper].add(
            jnp.einsum("hqk,qhd->kd", pround, gblock, preferred_element_type=jnp.float32)
        )
    back = jnp.stack([jnp.concatenate(outs, 0), jnp.concatenate(dqs, 0)]).reshape(
        2, shards, tok, per_dev * width
    )
    returned = lax.all_to_all(back, "sp", split_axis=1, concat_axis=3, tiled=True).reshape(
        2, tok, q_heads * width
    )
    kv_parts = jnp.stack([dkey, dval]).astype(jnp.bfloat16)
    picker = (jnp.arange(kv_heads, dtype=jnp.int32) == own_head).astype(jnp.float32)
    term = (kv_parts.astype(jnp.float32)[:, :, None, :] * picker[None, None, :, None]).reshape(
        2, seq, kv_heads * width
    )
    summed = lax.psum_scatter(
        term.astype(jnp.bfloat16), "sp", scatter_dimension=1, tiled=True
    ).astype(jnp.float32)
    dqn = returned[1].astype(jnp.float32).reshape(tok, q_heads, width)
    dkn = summed[0].reshape(tok, kv_heads, width)
    d_query = (
        norm_backward_pass(dqn, qhat, qrstd, q_gain)
        .astype(jnp.bfloat16)
        .reshape(tok, q_heads * width)
    )
    key_gradient = (
        norm_backward_pass(dkn, khat, krstd, k_gain)
        .astype(jnp.bfloat16)
        .reshape(tok, kv_heads * width)
    )
    d_key_value = jnp.stack([key_gradient, summed[1].astype(jnp.bfloat16)])
    gains = lax.psum((jnp.sum(dqn * qhat, (0, 1)), jnp.sum(dkn * khat, (0, 1))), ("grp", "sp"))
    return (returned[0], d_query, d_key_value, gains[0], gains[1])


def solution(mesh):
    placed = (
        P(("grp", "sp"), None),
        P(None, ("grp", "sp"), None),
        P(("grp", "sp"), None),
        P("grp", None, None),
        P("grp", None, None),
        P(),
        P(),
    )
    return jax.shard_map(
        local,
        mesh=mesh,
        in_specs=placed,
        out_specs=(
            P(("grp", "sp"), None),
            P(("grp", "sp"), None),
            P(None, ("grp", "sp"), None),
            P(),
            P(),
        ),
        check_vma=False,
    )
```

profile of v0, /device:TPU:1, one launch (start us, length us, event | category | flops | bytes accessed | tf_op | source)
XLA Modules:
  0.0 368.5 jit_solution(6237868827341984065)
XLA Ops:
  17.8 7.6 %all-to-all-start = ((bf16[2,128,16,256]{1,3,0,2:T(8,128)(2,1)}), bf16[2,128,16,256]{1,3,0,2:T(8,128)(2,1)}, u32[]{:S(2)}, u32[]{:S(2)}) async-start(bf16[2,128,16,256]{1,3,0,2:T(8,128)(2,1)} %copy.148), calls=%async_computation | async-start | bytes 4194304 | tf_op jit(solution)/shard_map/all_to_all | solution.py:47
  26.7 1.5 compare_and_fusion.1
  28.2 1.8 fusion.17
  30.0 2.2 compare_and_fusion
  32.2 25.6 %all-to-all-done = bf16[2,128,16,256]{1,3,0,2:T(8,128)(2,1)} async-done(((bf16[2,128,16,256]{1,3,0,2:T(8,128)(2,1)}), bf16[2,128,16,256]{1,3,0,2:T(8,128)(2,1)}, u32[]{:S(2)}, u32[]{:S(2)}) %all-to-all-start) | async-done | bytes 2097184 | tf_op jit(solution)/shard_map/all_to_all | solution.py:47
  57.8 2.5 fusion.131
  60.2 1.8 copy.149
  62.0 1.7 slice.321
  63.8 1.9 copy.177
  65.6 1.8 slice.355
  69.3 1.9 copy.169
  71.2 1.8 slice.351
  75.9 1.7 slice.347
  79.4 12.5 %all-gather.2.cloned.1.call-done = bf16[2,2048,512]{2,1,0:T(8,128)(2,1)} async-done(((bf16[2,128,512]{2,1,0:T(8,128)(2,1)}), bf16[2,2048,512]{2,1,0:T(8,128)(2,1)}) %all-gather.2.cloned.1.call-update) | async-done | bytes 4194320 | tf_op jit(solution)/shard_map/all_gather | solution.py:52
  92.0 3.3 fusion.146
  95.3 2.0 fusion.65
  97.8 2.0 multiply_reduce_fusion.6
  99.7 1.5 fusion.40
  103.8 4.8 %fusion.141 = (f32[2,512]{1,0:T(2,128)S(1)}, f32[2,512,1024]{1,2,0:T(8,128)}) fusion(pred[512,1024]{0,1:T(8,128)(4,1)} %compare_and_fusion.1, bf16[512,2,128]{2,1,0:T(2,128)(2,1)} %slice.331, bf16[2,2048,512]{2,1,0:T(8,128)(2,1)} %all-gather.2.cloned.1.call-done, s32[]{:T(128)S(6)} %select_n.28), kind=kOutput, calls=%fused_computation.204 | convolution fusion | flops 272630784 | bytes 5246980 | tf_op jit(solution)/shard_map/sub | solution.py:82
  108.5 2.9 fusion.45
  112.2 2.9 multiply_reduce_fusion.5
  115.1 1.7 fusion.14
  118.9 6.4 %fusion.138 = (f32[2,512]{1,0:T(2,128)S(1)}, f32[2,512,1536]{1,2,0:T(8,128)}) fusion(pred[512,1536]{0,1:T(8,128)(4,1)} %compare_and_fusion, bf16[2,2048,512]{2,1,0:T(8,128)(2,1)} %all-gather.2.cloned.1.call-done, s32[]{:T(128)S(6)} %select_n.28, bf16[512,2,128]{2,1,0:T(2,128)(2,1)} %slice.341), kind=kOutput, calls=%fused_computation.203 | convolution fusion | flops 408946176 | bytes 7737348 | tf_op jit(solution)/shard_map/sub | solution.py:82
  125.3 4.3 %fusion.24 = bf16[2,512,1536]{1,2,0:T(8,128)(2,1)S(1)} fusion(f32[2,512,1536]{1,2,0:T(8,128)} %get-tuple-element.159, f32[2,512]{1,0:T(2,128)S(1)} %get-tuple-element.158), kind=kLoop, calls=%fused_computation.38 | loop fusion | flops 3145728 | bytes 9441280 | tf_op jit(solution)/shard_map/convert_element_type | solution.py:83
  130.7 2.7 multiply_reduce_fusion.4
  133.4 2.2 fusion.10
  135.7 1.7 copy-done.4
  138.4 7.8 %fusion.133 = (f32[2,512]{1,0:T(2,128)S(1)}, f32[2,512,2048]{1,2,0:T(8,128)}) fusion(pred[512,2048]{0,1:T(8,128)(4,1)} %fusion.17, bf16[2,2048,512]{2,1,0:T(8,128)(2,1)} %all-gather.2.cloned.1.call-done, s32[]{:T(128)S(6)} %select_n.28, bf16[512,2,128]{2,1,0:T(2,128)(2,1)S(1)} %copy-done.27), kind=kOutput, calls=%fused_computation.202 | convolution fusion | flops 545261568 | bytes 10227716 | tf_op jit(solution)/shard_map/sub | solution.py:82
  146.3 4.8 %fusion.19 = bf16[2,512,2048]{1,2,0:T(8,128)(2,1)S(1)} fusion(f32[2,512,2048]{1,2,0:T(8,128)} %get-tuple-element.155, f32[2,512]{1,0:T(2,128)S(1)} %get-tuple-element.154), kind=kLoop, calls=%fused_computation.31 | loop fusion | flops 4194304 | bytes 12587008 | tf_op jit(solution)/shard_map/convert_element_type | solution.py:83
  152.4 1.8 multiply_reduce_fusion.3
  154.2 3.1 fusion.6
  159.5 4.1 %mul.361 = f32[2,2048,4,128]{3,2,1,0:T(4,128)} broadcast(f32[2,2048,128]{2,1,0:T(8,128)S(1)} %maximum_convert_fusion), dimensions={0,1,3} | broadcast | bytes 10485760 | tf_op jit(solution)/shard_map/mul | solution.py:110
  163.6 10.3 %mul.362 = f32[2,2048,512]{2,1,0:T(8,128)} reshape(f32[2,2048,4,128]{3,2,1,0:T(4,128)} %mul.361) | data formatting | bytes 16777216 | tf_op jit(solution)/shard_map/mul | solution.py:110
  173.8 6.5 %multiply_convert_fusion = bf16[2,2048,512]{2,1,0:T(8,128)(2,1)} fusion(f32[2,2048,512]{2,1,0:T(8,128)} %mul.362, f32[512]{0:T(512)S(1)} %broadcast_bitcast_fusion.1), kind=kLoop, calls=%fused_computation.9 | loop fusion | flops 4194304 | bytes 12584960 | tf_op jit(solution)/shard_map/convert_element_type | solution.py:114
  183.0 2.3 fusion.53
  185.3 1.6 fusion.57
  187.0 1.8 fusion.51
  190.6 1.5 pad_maximum_fusion.1
  192.1 5.3 %all-to-all-start.1 = ((bf16[2,16,128,256]{2,3,0,1:T(8,128)(2,1)}), bf16[2,16,128,256]{2,3,0,1:T(8,128)(2,1)}, u32[]{:S(2)}, u32[]{:S(2)}) async-start(bf16[2,16,128,256]{2,3,0,1:T(8,128)(2,1)} %pad_maximum_fusion.1), calls=%async_computation.1 | async-start | bytes 4194304 | tf_op jit(solution)/shard_map/all_to_all | solution.py:105
  197.4 2.9 copy.187
  200.3 30.0 %all-to-all-done.1 = bf16[2,16,128,256]{2,3,0,1:T(8,128)(2,1)} async-done(((bf16[2,16,128,256]{2,3,0,1:T(8,128)(2,1)}), bf16[2,16,128,256]{2,3,0,1:T(8,128)(2,1)}, u32[]{:S(2)}, u32[]{:S(2)}) %all-to-all-start.1) | async-done | bytes 2097184 | tf_op jit(solution)/shard_map/all_to_all | solution.py:105
  230.3 2.0 copy.282
  234.3 3.2 slice_convert_fusion
  238.8 2.9 copy.184
  241.7 2.2 multiply_reduce_fusion.1
  245.5 4.4 %fusion.37 = bf16[128,4096]{1,0:T(8,128)(2,1)} fusion(f32[128,4096]{1,0:T(8,128)S(1)} %copy-done.13, f32[16,8,32,128]{3,2,1,0:T(8,128)S(1)} %bitcast.346, f32[128,4096]{1,0:T(8,128)} %copy.184, f32[4096]{0:T(1024)S(1)} %broadcast_bitcast_fusion, bf16[128,4096]{1,0:T(8,128)(2,1)S(1)} %copy-done.17), kind=kLoop, calls=%fused_computation.56 | loop fusion | flops 3670016 | bytes 8404992 | tf_op jit(solution)/shard_map/convert_element_type | solution.py:120
  249.8 29.8 %reduce-scatter.2.cloned.1.call-done = bf16[2,128,512]{2,1,0:T(8,128)(2,1)} async-done(((bf16[2,2048,512]{2,1,0:T(8,128)(2,1)}), bf16[2,128,512]{2,1,0:T(8,128)(2,1)}) %reduce-scatter.2.cloned.1.call-update) | async-done | bytes 262160 | tf_op jit(solution)/shard_map/reduce_scatter | solution.py:113
  283.5 77.2 %all-reduce.2 = (f32[128]{0:T(128)}, f32[128]{0:T(128)}) all-reduce(f32[128]{0:T(128)S(1)} %reduce_sum.164, f32[128]{0:T(128)S(1)} %bitcast_reduce_fusion), channel_id=1, replica_groups=mesh['grp'=16,'sp'=16] {'grp','sp'}, use_global_device_ids=true, to_apply=%region_20.21 | all-reduce | flops 256 | bytes 2048 | tf_op jit(solution)/shard_map/psum | solution.py:129
  (167 shorter events, 43.1 us)
Async XLA Ops:
  7.2 4.8 %copy-start.37 = (s32[1,1,16]{2,1,0:T(1,128)S(1)}, s32[1,1,16]{2,1,0:T(1,128)}, u32[]{:S(2)}) copy-start(s32[1,1,16]{2,1,0:T(1,128)} %param.31) | copy-start | bytes 196
  7.2 4.8 %copy-start.34 = (s32[1,1,2048]{2,1,0:T(1,128)S(1)}, s32[1,1,2048]{2,1,0:T(1,128)}, u32[]{:S(2)}) copy-start(s32[1,1,2048]{2,1,0:T(1,128)} %param.30) | copy-start | bytes 24580
  7.2 5.0 %copy-start.26 = (bf16[128,4096]{1,0:T(8,128)(2,1)S(1)}, bf16[128,4096]{1,0:T(8,128)(2,1)}, u32[]{:S(2)}) copy-start(bf16[128,4096]{1,0:T(8,128)(2,1)} %param.29) | copy-start | bytes 3145732
  7.2 84.8 %all-gather.2.cloned.1.call-start = ((), (), s32[]{:S(2)}) async-start(), calls=%async_computation.3 | async-start | bytes 4456448 | tf_op jit(solution)/shard_map/all_gather | solution.py:52
  9.1 0.7 copy-start.21
  10.1 2.0 copy-start.19
  13.1 1.7 copy-start.35
  14.9 1.4 copy-start
  17.8 39.9 %all-to-all-start = ((bf16[2,128,16,256]{1,3,0,2:T(8,128)(2,1)}), bf16[2,128,16,256]{1,3,0,2:T(8,128)(2,1)}, u32[]{:S(2)}, u32[]{:S(2)}) async-start(bf16[2,128,16,256]{1,3,0,2:T(8,128)(2,1)} %copy.148), calls=%async_computation | async-start | bytes 4194304 | tf_op jit(solution)/shard_map/all_to_all | solution.py:47
  25.5 254.1 %reduce-scatter.2.cloned.1.call-start = ((), (), s32[]{:S(2)}) async-start(), calls=%async_computation.4 | async-start | bytes 4456448 | tf_op jit(solution)/shard_map/reduce_scatter | solution.py:113
  75.0 22.7 %copy-start.23 = (bf16[512,2,128]{0,2,1:T(8,128)(2,1)}, bf16[512,2,128]{0,2,1:T(8,128)(2,1)S(1)}, u32[]{:S(2)}) copy-start(bf16[512,2,128]{0,2,1:T(8,128)(2,1)S(1)} %slice.349) | copy-start | bytes 786436
  95.3 4.4 %copy-start.25 = (f32[2,512,512]{1,2,0:T(8,128)S(1)}, f32[2,512,512]{1,2,0:T(8,128)}, u32[]{:S(2)}) copy-start(f32[2,512,512]{1,2,0:T(8,128)} %get-tuple-element.167) | copy-start | bytes 6291460
  99.7 2.5 copy-start.30
  101.2 1.0 copy-start.15
  108.5 2.9 copy-start.6
  108.5 2.9 copy-start.24
  111.4 3.6 copy-start.14
  112.2 4.7 %copy-start.7 = (f32[2048,128]{1,0:T(8,128)}, f32[2048,128]{1,0:T(8,128)S(1)}, u32[]{:S(2)}) copy-start(f32[2048,128]{1,0:T(8,128)S(1)} %fusion.49) | copy-start | bytes 3145732
  115.1 3.1 copy-start.31
  116.8 1.3 copy-start.12
  125.3 4.4 %copy-start.8 = (f32[2048,128]{1,0:T(8,128)S(1)}, f32[2048,128]{1,0:T(8,128)}, u32[]{:S(2)}) copy-start(f32[2048,128]{1,0:T(8,128)} %copy-done.7) | copy-start | bytes 3145732
  125.3 8.0 %slice-start.2 = ((s8[6291456]{0:T(1024)(128)(4,1)}), s8[4194304]{0:T(1024)(128)(4,1)S(1)}, s32[]{:S(2)}) async-start(s8[6291456]{0:T(1024)(128)(4,1)} %bitcast.347), calls=%async_computation.7 | async-start | bytes 8388608
  129.7 3.7 %slice-start.3 = ((s8[6291456]{0:T(1024)(128)(4,1)}), s8[2097152]{0:T(1024)(128)(4,1)S(1)}, s32[]{:S(2)}) async-start(s8[6291456]{0:T(1024)(128)(4,1)} %bitcast.347), calls=%async_computation.8 | async-start | bytes 4194304
  130.7 4.9 %copy-start.9 = (f32[2048,128]{1,0:T(8,128)}, f32[2048,128]{1,0:T(8,128)S(1)}, u32[]{:S(2)}) copy-start(f32[2048,128]{1,0:T(8,128)S(1)} %fusion.28) | copy-start | bytes 3145732
  133.4 4.0 %copy-start.29 = (bf16[512,2,128]{2,1,0:T(2,128)(2,1)S(1)}, bf16[512,2,128]{2,1,0:T(2,128)(2,1)}, u32[]{:S(2)}) copy-start(bf16[512,2,128]{2,1,0:T(2,128)(2,1)} %slice.341) | copy-start | bytes 786436
  135.6 1.8 copy-start.4
  137.4 1.0 copy-start.27
  146.2 4.8 %copy-start.10 = (f32[2048,128]{1,0:T(8,128)S(1)}, f32[2048,128]{1,0:T(8,128)}, u32[]{:S(2)}) copy-start(f32[2048,128]{1,0:T(8,128)} %copy-done.9) | copy-start | bytes 3145732
  146.2 4.8 %copy-start.18 = (bf16[512,2,128]{0,2,1:T(8,128)(2,1)S(1)}, bf16[512,2,128]{0,2,1:T(8,128)(2,1)}, u32[]{:S(2)}) copy-start(bf16[512,2,128]{0,2,1:T(8,128)(2,1)} %slice.355) | copy-start | bytes 786436
  146.3 8.0 %slice-start = ((s8[8388608]{0:T(1024)(128)(4,1)}), s8[4194304]{0:T(1024)(128)(4,1)S(1)}, s32[]{:S(2)}) async-start(s8[8388608]{0:T(1024)(128)(4,1)} %bitcast.344), calls=%async_computation.5 | async-start | bytes 8388608
  151.1 3.2 slice-start.1
  154.2 3.1 copy-start.28
  157.4 2.0 copy-start.2
  180.4 1.2 copy-start.16
  181.6 3.7 %copy-start.5 = (bf16[2,512,1536]{1,2,0:T(8,128)(2,1)S(1)}, bf16[2,512,1536]{1,2,0:T(8,128)(2,1)}, u32[]{:S(2)}) copy-start(bf16[2,512,1536]{1,2,0:T(8,128)(2,1)} %copy-done.4) | copy-start | bytes 9437188
  183.0 4.0 %copy-start.3 = (bf16[2,512,2048]{1,2,0:T(8,128)(2,1)S(1)}, bf16[2,512,2048]{1,2,0:T(8,128)(2,1)}, u32[]{:S(2)}) copy-start(bf16[2,512,2048]{1,2,0:T(8,128)(2,1)} %copy-done.2) | copy-start | bytes 12582916
  188.8 1.0 copy-start.22
  188.8 1.0 copy-start.32
  188.8 1.1 copy-start.33
  192.1 38.2 %all-to-all-start.1 = ((bf16[2,16,128,256]{2,3,0,1:T(8,128)(2,1)}), bf16[2,16,128,256]{2,3,0,1:T(8,128)(2,1)}, u32[]{:S(2)}, u32[]{:S(2)}) async-start(bf16[2,16,128,256]{2,3,0,1:T(8,128)(2,1)} %pad_maximum_fusion.1), calls=%async_computation.1 | async-start | bytes 4194304 | tf_op jit(solution)/shard_map/all_to_all | solution.py:105
  230.3 3.3 copy-start.1
  232.2 1.3 copy-start.11
  241.7 2.9 copy-start.17
  243.9 1.6 copy-start.13
  245.5 35.2 %copy-start.36 = (f32[128]{0:T(128)S(1)}, f32[128]{0:T(128)}, u32[]{:S(2)}) copy-start(f32[128]{0:T(128)} %param.33) | copy-start | bytes 1540
  245.5 36.9 %copy-start.20 = (f32[1,128,512]{2,1,0:T(8,128)S(1)}, f32[1,128,512]{2,1,0:T(8,128)}, u32[]{:S(2)}) copy-start(f32[1,128,512]{2,1,0:T(8,128)} %copy-done.19) | copy-start | bytes 786436
Sparse Core Ops, SparseCore 0:
  12.0 79.8 all-gather.1
  180.5 99.0 reduce-scatter.1
where the time goes:
time: 374 us; the launch traced here: 368 us
  waiting for transfers between devices  97.9 us (26%)
  blocking collectives  77.2 us (21%)
  local copies, waits for them, and re-layouts  63.2 us (17%)
  matrix products  54.3 us (15%)
  other arithmetic  47.7 us (13%)
  between operations  15.2 us (4%)
  starting transfers between devices  13 us (3%)
    psum x1, blocking collectives, local(): lax.psum((jnp.sum(dqn * qhat, (0, 1)), jnp.sum(dkn * khat, (0, 1))), ('gr...  77.2 us
    all_to_all x1, waiting for transfers between devices, local(): lax.all_to_all(back, 'sp', split_axis=1, concat_axis=3, tiled=True)  30 us
    reduce_scatter x1, waiting for transfers between devices, local(): lax.psum_scatter(term.astype(jnp.bfloat16), 'sp', scatter_dimension=1, ti...  29.8 us
    all_to_all x1, waiting for transfers between devices, local(): lax.all_to_all(stacked, 'sp', split_axis=2, concat_axis=1, tiled=True)  25.6 us
    sub x4, matrix products, local(): prob = jax.nn.softmax(scores, -1)  22.3 us
    mul x3, local copies, waits for them, and re-layouts, local(): kv_parts.astype(jnp.float32)[:, :, None, :] * picker[None, None, :, None]  14.4 us
    convert_element_type x4, other arithmetic, local(): pround = prob.astype(jnp.bfloat16)  14 us
    all_gather x1, waiting for transfers between devices, local(): full = lax.all_gather(pair, 'sp', axis=1, tiled=True)  12.5 us
  transfers between devices with their start and end apart: 4, of which 4 were waited for; matrix products, arithmetic and copies ran while one was open for 17% of the time, Pallas kernels for 0%

commit v1 on v0

v1 whole, which is shorter than its diff:
```python
import functools
import math

import jax
import jax.numpy as jnp
from jax import lax
from jax.experimental import pallas as pl
from jax.experimental.pallas import tpu as pltpu
from jax.sharding import Mesh, PartitionSpec as P

EPS = 1e-06
LOG2E = math.log2(math.e)
ROWS = (((0,), (0,)), ((), ()))
LAST = (((1,), (1,)), ((), ()))
MIB = 2**20


def rms_parts(x):
    inverse = lax.rsqrt(jnp.mean(x * x, -1, keepdims=True) + EPS)
    return x * inverse, inverse


def attention_kernel(
    axis, q_ref, g_ref, own_ref, one_ref, two_ref, seg_ref, lag_ref, qg_ref, kg_ref, *rest
):
    out_ref, dq_ref, d_own_ref, d_one_ref, d_two_ref, gain_ref, bias, coef = rest[-8:]
    before = rest[:-8]
    tok, wide = q_ref.shape
    width = qg_ref.shape[1]
    heads = wide // width
    scale = width ** (-0.5)

    @pl.when(pl.program_id(0) == 0)
    def _():
        rank = lax.axis_index(axis)

        def seg_block(back):
            start = pl.multiple_of(jnp.maximum(rank - back, 0) * tok, tok)
            row = jnp.broadcast_to(seg_ref[0, :, pl.ds(start, tok)], (tok, tok))
            return jnp.where(rank >= back, row, -1)

        mine = seg_block(0)
        seg_q = mine.T
        row = lax.broadcasted_iota(jnp.int32, (tok, tok), 0)
        col = lax.broadcasted_iota(jnp.int32, (tok, tok), 1)
        bias[:, 0:tok] = jnp.where((mine == seg_q) & (col <= row), 0.0, -1e30)
        bias[:, tok : 2 * tok] = jnp.where(seg_block(1) == seg_q, 0.0, -1e30)
        bias[:, 2 * tok : 3 * tok] = jnp.where(seg_block(2) == seg_q, 0.0, -1e30)
        late = jnp.zeros((tok, tok), jnp.int32)
        for r in range(lag_ref.shape[2]):
            late = jnp.where(seg_q == r, lag_ref[0, 0, r], late)
        coef[...] = 8.0 / (8.0 + late.astype(jnp.float32))
        gain_ref[...] = before[-1][...] if before else jnp.zeros_like(gain_ref)

    def stack(ref):
        return jnp.concatenate(
            [ref[:, h * width : (h + 1) * width].astype(jnp.float32) for h in range(heads)], 0
        )

    def spread(tile):
        return jnp.concatenate([tile] * heads, 0)

    q_gain = qg_ref[...]
    k_gain = kg_ref[...]
    qhat, qr = rms_parts(stack(q_ref))
    qs = (qhat * (q_gain * (scale * LOG2E))).astype(jnp.bfloat16)
    khat, _ = rms_parts(
        jnp.concatenate([ref[0].astype(jnp.float32) for ref in (own_ref, one_ref, two_ref)], 0)
    )
    kn = (khat * k_gain).astype(jnp.bfloat16)
    v = jnp.concatenate([ref[1] for ref in (own_ref, one_ref, two_ref)], 0)
    s = lax.dot_general(qs, kn, LAST, preferred_element_type=jnp.float32)
    p = jnp.exp2(s + spread(bias[...]))
    pb = p.astype(jnp.bfloat16)
    inv = 1.0 / jnp.sum(p, -1, keepdims=True)
    out = jnp.dot(pb, v, preferred_element_type=jnp.float32) * inv
    grad = stack(g_ref) * spread(coef[...]) * inv
    gb = grad.astype(jnp.bfloat16)
    delta = jnp.sum(grad * out, -1, keepdims=True)
    dp = lax.dot_general(gb, v, LAST, preferred_element_type=jnp.float32)
    ds = (p * (dp - delta)).astype(jnp.bfloat16)
    dqn = jnp.dot(ds, kn, preferred_element_type=jnp.float32) * scale
    dk = lax.dot_general(ds, qs, ROWS, preferred_element_type=jnp.float32) * (1.0 / LOG2E)
    dv = lax.dot_general(pb, gb, ROWS, preferred_element_type=jnp.float32)
    gain_ref[...] += jnp.sum(dqn * qhat, 0, keepdims=True)
    up = dqn * q_gain
    dq = qr * (up - qhat * jnp.mean(up * qhat, -1, keepdims=True))
    for h in range(heads):
        at = slice(h * width, (h + 1) * width)
        rows = slice(h * tok, (h + 1) * tok)
        out_ref[:, at] = out[rows].astype(jnp.bfloat16)
        dq_ref[:, at] = dq[rows].astype(jnp.bfloat16)
    for i, ref in enumerate((d_own_ref, d_one_ref, d_two_ref)):
        rows = slice(i * tok, (i + 1) * tok)
        ref[0] = dk[rows].astype(jnp.bfloat16)
        ref[1] = dv[rows].astype(jnp.bfloat16)


def finish_kernel(
    kv_ref, own_ref, one_ref, two_ref, parts_ref, qg_ref, kg_ref, out_ref, q_gain_ref, k_gain_ref
):
    width = kg_ref.shape[1]
    gain = kg_ref[...]
    total_gain = jnp.sum(parts_ref[...], 0, keepdims=True)
    q_gain_ref[...] = total_gain
    k_gain_ref[...] = total_gain * qg_ref[...] / gain
    for h in range(kv_ref.shape[2] // width):
        at = slice(h * width, (h + 1) * width)

        def total(i):
            return (
                own_ref[i, :, at].astype(jnp.float32)
                + one_ref[i, :, at].astype(jnp.float32)
                + two_ref[i, :, at].astype(jnp.float32)
            )

        khat, kr = rms_parts(kv_ref[0, :, at].astype(jnp.float32))
        up = total(0) * gain
        dk = kr * (up - khat * jnp.mean(up * khat, -1, keepdims=True))
        out_ref[0, :, at] = dk.astype(jnp.bfloat16)
        out_ref[1, :, at] = total(1).astype(jnp.bfloat16)


def attention(first, query, grad_out, key_value, one, two, segment_ids, lag, q_gain, k_gain, before):
    tok, wide = query.shape
    width = q_gain.shape[1]
    kv_heads = key_value.shape[2] // width
    number = one.shape[2] // width
    part = wide // kv_heads
    q_spec = pl.BlockSpec((tok, part), lambda g: (0, g + first))
    kv_spec = pl.BlockSpec((2, tok, width), lambda g: (0, 0, g + first))
    halo_spec = pl.BlockSpec((2, tok, width), lambda g: (0, 0, g))
    whole = lambda a: pl.BlockSpec(a.shape, lambda g: (0,) * a.ndim)
    kept = jax.ShapeDtypeStruct(key_value.shape, jnp.bfloat16)
    rows = jax.ShapeDtypeStruct(query.shape, jnp.bfloat16)
    any_spec = pl.BlockSpec(memory_space=pl.ANY)
    vector = pl.BlockSpec((1, width), lambda g: (0, 0))
    operands = (query, grad_out, key_value, one, two, segment_ids, lag, q_gain, k_gain)
    return pl.pallas_call(
        functools.partial(attention_kernel, "sp"),
        grid=(number,),
        in_specs=[
            q_spec, q_spec, kv_spec, halo_spec, halo_spec, whole(segment_ids),
            pl.BlockSpec(memory_space=pltpu.SMEM), whole(q_gain), whole(k_gain),
        ] + ([any_spec] * 5 + [vector] if before else []),
        out_specs=[q_spec, q_spec, kv_spec, kv_spec, kv_spec, vector],
        out_shape=[rows, rows, kept, kept, kept, jax.ShapeDtypeStruct((1, width), jnp.float32)],
        input_output_aliases={len(operands) + i: i for i in range(len(before))},
        scratch_shapes=[
            pltpu.VMEM((tok, 3 * tok), jnp.float32),
            pltpu.VMEM((tok, tok), jnp.float32),
        ],
        compiler_params=pltpu.CompilerParams(vmem_limit_bytes=60 * MIB),
        cost_estimate=pl.CostEstimate(
            flops=36 * tok * tok * part * number, bytes_accessed=8 * tok * part * number,
            transcendentals=3 * tok * tok * part * number // width,
        ),
        name=f"attention{first}",
    )(*operands, *before)


def finish(key_value, own, one, two, parts, q_gain, k_gain):
    vector = jax.ShapeDtypeStruct(k_gain.shape, jnp.float32)
    return pl.pallas_call(
        finish_kernel,
        out_shape=[jax.ShapeDtypeStruct(key_value.shape, jnp.bfloat16), vector, vector],
        compiler_params=pltpu.CompilerParams(vmem_limit_bytes=16 * MIB),
        name="finish",
    )(key_value, own, one, two, parts, q_gain, k_gain)


def local(query, key_value, grad_out, segment_ids, lag, q_gain, k_gain):
    shards = lax.axis_size("sp")
    width = q_gain.shape[0]
    q_gain = q_gain.reshape(1, width)
    k_gain = k_gain.reshape(1, width)

    def shift(x, by):
        return lax.ppermute(x, "sp", [(i, (i + by) % shards) for i in range(shards)])

    one = shift(key_value, 1)
    two = shift(key_value, 2)
    out, d_query, d_own, d_one, d_two, gain = attention(
        0, query, grad_out, key_value, one, two, segment_ids, lag, q_gain, k_gain, ()
    )
    d_one = shift(d_one, -1)
    d_two = shift(d_two, -2)
    gain = gain + lax.ppermute(gain, "core", [(0, 1), (1, 0)])
    chips = ("chip", "sp")
    copies = jnp.broadcast_to(gain, (lax.axis_size(chips), width))
    parts = lax.all_to_all(copies, chips, 0, 0, tiled=True)
    d_key_value, d_q_gain, d_k_gain = finish(
        key_value, d_own, d_one, d_two, parts, q_gain, k_gain
    )
    return out, d_query, d_key_value, d_q_gain.reshape(width), d_k_gain.reshape(width)


def solution(mesh):
    groups, shards = mesh.devices.shape
    mesh = Mesh(mesh.devices.reshape(groups // 2, 2, shards), ("chip", "core", "sp"))
    tokens = P(("chip", "core", "sp"), None)
    pair = P(None, ("chip", "core", "sp"), None)
    group = P(("chip", "core"), None, None)
    return jax.shard_map(
        local,
        mesh=mesh,
        in_specs=(tokens, pair, tokens, group, group, P(), P()),
        out_specs=(tokens, tokens, pair, P(), P()),
        check_vma=False,
    )
```

time: 374 us -> 58.9 us (0.16); the launches traced: 368 us -> 58.7 us
  waiting for transfers between devices: 97.9 us -> 14 us
  local copies, waits for them, and re-layouts: 63.2 us -> 3 us
  matrix products: 54.3 us -> 0 us
  blocking collectives: 77.2 us -> 23.2 us
  other arithmetic: 47.7 us -> 0.01 us
  between operations: 15.2 us -> 0.67 us
  Pallas kernels: 0 us -> 9.45 us
  starting transfers between devices: 13 us -> 8.37 us
    psum x1 -> x0, blocking collectives: 77.2 us -> none  [local(): lax.psum((jnp.sum(dqn * qhat, (0, 1)), jnp.sum(dkn * khat, (0, 1))), ('gr...]
    all_to_all x2 -> x0, waiting for transfers between devices: 55.5 us -> none  [the longest x1 30 us: local(): lax.all_to_all(back, 'sp', split_axis=1, concat_axis=3, tiled=True)]
    dot_general x20 -> x0, matrix products: 32 us -> none  [the longest x4 9.34 us: local(): jnp.einsum('hqk,kd->qhd', pround, vpart, preferred_element_type=jnp.float32)]
    convert_element_type x13 -> x0, other arithmetic: 30.9 us -> none  [the longest x4 14 us: local(): pround = prob.astype(jnp.bfloat16)]
    reduce_scatter x1 -> x0, waiting for transfers between devices: 29.8 us -> none  [local(): lax.psum_scatter(term.astype(jnp.bfloat16), 'sp', scatter_dimension=1, ti...]
    all_to_all x0 -> x1, blocking collectives: none -> 23.2 us  [local(): parts = lax.all_to_all(copies, chips, 0, 0, tiled=True)]
    sub x4 -> x0, matrix products: 22.3 us -> none  [local(): prob = jax.nn.softmax(scores, -1)]
    slice x20 -> x0, local copies, waits for them, and re-layouts: 21.6 us -> none  [the longest x8 11.2 us: local(): gblock = g_side[lower:upper]]
  transfers between devices with their start and end apart: 4 -> 5, of which waited for: 4 -> 2; matrix products, arithmetic and copies ran while one was open for 17% -> 0% of each run, Pallas kernels for 0% -> 0%
where the time goes in v1:
time: 58.9 us; the launch traced here: 58.7 us
  blocking collectives  23.2 us (39%)
  waiting for transfers between devices  14 us (24%)
  Pallas kernels  9.45 us (16%)
  starting transfers between devices  8.37 us (14%)
  local copies, waits for them, and re-layouts  3 us (5%)
  between operations  0.67 us (1%)
    all_to_all x1, blocking collectives, local(): parts = lax.all_to_all(copies, chips, 0, 0, tiled=True)  23.2 us
    ppermute x4, waiting for transfers between devices, shift(): lax.ppermute(x, 'sp', [(i, (i + by) % shards) for i in range(shards)])  14 us
    pallas_call x1, Pallas kernels, attention(): pl.pallas_call(functools.partial(attention_kernel, 'sp'), grid=(number,),...  8.45 us
    ppermute x4, starting transfers between devices, shift(): lax.ppermute(x, 'sp', [(i, (i + by) % shards) for i in range(shards)])  6.82 us
    unnamed x14, local copies, waits for them, and re-layouts  2.96 us
    ppermute x1, starting transfers between devices, local(): gain = gain + lax.ppermute(gain, 'core', [(0, 1), (1, 0)])  1.55 us
  transfers between devices with their start and end apart: 5, of which 2 were waited for; matrix products, arithmetic and copies ran while one was open for 0% of the time, Pallas kernels for 0%

profile of v1, /device:TPU:1, one launch (start us, length us, event | category | flops | bytes accessed | tf_op | source)
XLA Modules:
  0.0 58.7 jit_solution(2530973741036773183)
XLA Ops:
  0.6 3.8 %collective-permute-start.1 = (bf16[2,128,512]{2,1,0:T(8,128)(2,1)}, bf16[2,128,512]{2,1,0:T(8,128)(2,1)S(1)}, u32[]{:S(2)}, u32[]{:S(2)}) collective-permute-start(bf16[2,128,512]{2,1,0:T(8,128)(2,1)} %kv_ref.1), channel_id=1, source_target_pairs={{0,2},{1,3},{2,4},{3,5},{4,6},{5,7},{6,8},{7,9},{8,10},{9,11},{10,... | collective-permute-start | bytes 786440 | tf_op jit(solution)/shard_map/ppermute | solution.py:179
  4.5 0.4 collective-permute-start
  4.9 5.9 %collective-permute-done.1.two_ref = bf16[2,128,512]{2,1,0:T(8,128)(2,1)S(1)} collective-permute-done((bf16[2,128,512]{2,1,0:T(8,128)(2,1)}, bf16[2,128,512]{2,1,0:T(8,128)(2,1)S(1)}, u32[]{:S(2)}, u32[]{:S(2)}) %collective-permute-start.1) | collective-permute-done | bytes 262176 | tf_op jit(solution)/shard_map/ppermute | solution.py:179
  10.7 0.0 copy-start.4
  10.7 8.2 %collective-permute-done.one_ref = bf16[2,128,512]{2,1,0:T(8,128)(2,1)S(1)} collective-permute-done((bf16[2,128,512]{2,1,0:T(8,128)(2,1)}, bf16[2,128,512]{2,1,0:T(8,128)(2,1)S(1)}, u32[]{:S(2)}, u32[]{:S(2)}) %collective-permute-start) | collective-permute-done | bytes 262176 | tf_op jit(solution)/shard_map/ppermute | solution.py:179
  18.9 0.0 copy-start.5
  18.9 0.0 copy-done.4
  18.9 0.7 %copy-done.5 = bf16[2,128,512]{2,1,0:T(8,128)(2,1)} copy-done((bf16[2,128,512]{2,1,0:T(8,128)(2,1)}, bf16[2,128,512]{2,1,0:T(8,128)(2,1)S(1)}, u32[]{:S(2)}) %copy-start.5) | copy-done | bytes 262168
  19.6 0.0 copy-start
  19.6 8.5 %attention0.1 = (bf16[128,4096]{1,0:T(8,128)(2,1)}, bf16[128,4096]{1,0:T(8,128)(2,1)}, bf16[2,128,512]{2,1,0:T(8,128)(2,1)}, bf16[2,128,512]{2,1,0:T(8,128)(2,1)...) custom-call(bf16[128,4096]{1,0:T(8,128)(2,1)} %q_ref.1, bf16[128,4096]{1,0:T(8,128)(2,1)} %g_ref.1, ...), custom_call_target="tpu_custom_call" | custom-call | flops 2415919104 | bytes 4194304 | tf_op jit(solution)/shard_map/attention0/pallas_call | solution.py:139
  28.0 0.0 copy-start.6
  28.0 0.6 %copy-done.6 = f32[1,128]{1,0:T(1,128)S(1)} copy-done((f32[1,128]{1,0:T(1,128)S(1)}, f32[1,128]{1,0:T(1,128)}, u32[]{:S(2)}) %copy-start.6) | copy-done | bytes 536
  28.7 1.5 %collective-permute-start.4 = (f32[1,128]{1,0:T(1,128)S(1)}, f32[1,128]{1,0:T(1,128)S(1)}, u32[]{:S(2)}, u32[]{:S(2)}) collective-permute-start(f32[1,128]{1,0:T(1,128)S(1)} %copy-done.6), channel_id=1, source_target_pairs={{0,16},{16,0},{1,17},{17,1},{2,18},{18,2},{3,19},{19,3},{4,20},{20... | collective-permute-start | bytes 1544 | tf_op jit(solution)/shard_map/ppermute | solution.py:188
  30.2 0.6 collective-permute-start.2
  30.8 2.1 %collective-permute-start.3 = (bf16[2,128,512]{2,1,0:T(8,128)(2,1)}, bf16[2,128,512]{2,1,0:T(8,128)(2,1)S(1)}, u32[]{:S(2)}, u32[]{:S(2)}) collective-permute-start(bf16[2,128,512]{2,1,0:T(8,128)(2,1)} %get-tuple-element.18), channel_id=1, source_target_pairs={{0,14},{1,15},{2,0},{3,1},{4,2},{5,3},{6,4},{7,5},{8,6},{9,7},{10,... | collective-permute-start | bytes 786440 | tf_op jit(solution)/shard_map/ppermute | solution.py:179
  32.8 0.0 collective-permute-done.4
  32.9 23.2 %all_to_all.8 = f32[128,1,128]{2,1,0:T(1,128)S(1)} all-to-all(f32[128,1,128]{2,1,0:T(1,128)S(1)} %broadcast_in_dim.2), channel_id=1, replica_groups=mesh['chip'=8,'core'=2,'sp'=16] {'chip','sp'}, dimensions={0} | all-to-all | bytes 131072 | tf_op jit(solution)/shard_map/all_to_all | solution.py:191
  56.1 0.0 collective-permute-done.2.one_ref
  56.1 0.0 collective-permute-done.3.two_ref
  56.1 0.0 copy-start.2
  56.1 0.0 copy-start.3
  56.1 0.0 copy-done
  56.1 0.6 %copy-done.2 = f32[128]{0:T(128)S(1)} copy-done((f32[128]{0:T(128)S(1)}, f32[128]{0:T(128)}, u32[]{:S(2)}) %copy-start.2) | copy-done | bytes 536
  56.7 0.0 copy-done.3
  56.7 0.0 copy-start.1
  56.8 0.9 %copy-done.1 = bf16[2,128,512]{2,1,0:T(8,128)(2,1)S(1)} copy-done((bf16[2,128,512]{2,1,0:T(8,128)(2,1)S(1)}, bf16[2,128,512]{2,1,0:T(8,128)(2,1)}, u32[]{:S(2)}) %copy-start.1) | copy-done | bytes 262168
  57.7 1.0 %finish.1 = (bf16[2,128,512]{2,1,0:T(8,128)(2,1)}, f32[1,128]{1,0:T(1,128)}, f32[1,128]{1,0:T(1,128)}) custom-call(bf16[2,128,512]{2,1,0:T(8,128)(2,1)S(1)} %copy-done, bf16[2,128,512]{2,1,0:T(8,128)(2,1)S(1)} %copy-done.1, bf16[2,128,512]{2,1,0:T(8,128)(2,1)S(1)} %collective-permute-done.2.one_ref, bf16[2,128,512]{2,1,0:T(8,128)(2,1)S(1)} %collective-permute-done.3.two_ref, ...), custom_call_target="tpu_custom_call" | custom-call | tf_op jit(solution)/shard_map/finish/pallas_call | solution.py:164
  (2 shorter events, 0.0 us)
Async XLA Ops:
  0.6 10.1 %collective-permute-start.1 = (bf16[2,128,512]{2,1,0:T(8,128)(2,1)}, bf16[2,128,512]{2,1,0:T(8,128)(2,1)S(1)}, u32[]{:S(2)}, u32[]{:S(2)}) collective-permute-start(bf16[2,128,512]{2,1,0:T(8,128)(2,1)} %kv_ref.1), channel_id=1, source_target_pairs={{0,2},{1,3},{2,4},{3,5},{4,6},{5,7},{6,8},{7,9},{8,10},{9,11},{10,... | collective-permute-start | bytes 786440 | tf_op jit(solution)/shard_map/ppermute | solution.py:179
  4.5 14.4 %collective-permute-start = (bf16[2,128,512]{2,1,0:T(8,128)(2,1)}, bf16[2,128,512]{2,1,0:T(8,128)(2,1)S(1)}, u32[]{:S(2)}, u32[]{:S(2)}) collective-permute-start(bf16[2,128,512]{2,1,0:T(8,128)(2,1)} %kv_ref.1), channel_id=1, source_target_pairs={{0,1},{1,2},{2,3},{3,4},{4,5},{5,6},{6,7},{7,8},{8,9},{9,10},{10,1... | collective-permute-start | bytes 786440 | tf_op jit(solution)/shard_map/ppermute | solution.py:179
  10.7 8.2 %copy-start.4 = (bf16[2,128,512]{2,1,0:T(8,128)(2,1)}, bf16[2,128,512]{2,1,0:T(8,128)(2,1)S(1)}, u32[]{:S(2)}) copy-start(bf16[2,128,512]{2,1,0:T(8,128)(2,1)S(1)} %collective-permute-done.1.two_ref) | copy-start | bytes 786436
  18.9 0.7 %copy-start.5 = (bf16[2,128,512]{2,1,0:T(8,128)(2,1)}, bf16[2,128,512]{2,1,0:T(8,128)(2,1)S(1)}, u32[]{:S(2)}) copy-start(bf16[2,128,512]{2,1,0:T(8,128)(2,1)S(1)} %collective-permute-done.one_ref) | copy-start | bytes 786436
  19.6 36.5 %copy-start = (bf16[2,128,512]{2,1,0:T(8,128)(2,1)S(1)}, bf16[2,128,512]{2,1,0:T(8,128)(2,1)}, u32[]{:S(2)}) copy-start(bf16[2,128,512]{2,1,0:T(8,128)(2,1)} %kv_ref.1) | copy-start | bytes 786436
  28.0 0.7 %copy-start.6 = (f32[1,128]{1,0:T(1,128)S(1)}, f32[1,128]{1,0:T(1,128)}, u32[]{:S(2)}) copy-start(f32[1,128]{1,0:T(1,128)} %get-tuple-element.19) | copy-start | bytes 1540
  28.7 4.2 %collective-permute-start.4 = (f32[1,128]{1,0:T(1,128)S(1)}, f32[1,128]{1,0:T(1,128)S(1)}, u32[]{:S(2)}, u32[]{:S(2)}) collective-permute-start(f32[1,128]{1,0:T(1,128)S(1)} %copy-done.6), channel_id=1, source_target_pairs={{0,16},{16,0},{1,17},{17,1},{2,18},{18,2},{3,19},{19,3},{4,20},{20... | collective-permute-start | bytes 1544 | tf_op jit(solution)/shard_map/ppermute | solution.py:188
  30.2 25.8 %collective-permute-start.2 = (bf16[2,128,512]{2,1,0:T(8,128)(2,1)}, bf16[2,128,512]{2,1,0:T(8,128)(2,1)S(1)}, u32[]{:S(2)}, u32[]{:S(2)}) collective-permute-start(bf16[2,128,512]{2,1,0:T(8,128)(2,1)} %get-tuple-element.17), channel_id=1, source_target_pairs={{0,15},{1,0},{2,1},{3,2},{4,3},{5,4},{6,5},{7,6},{8,7},{9,8},{10,9... | collective-permute-start | bytes 786440 | tf_op jit(solution)/shard_map/ppermute | solution.py:179
  30.8 25.3 %collective-permute-start.3 = (bf16[2,128,512]{2,1,0:T(8,128)(2,1)}, bf16[2,128,512]{2,1,0:T(8,128)(2,1)S(1)}, u32[]{:S(2)}, u32[]{:S(2)}) collective-permute-start(bf16[2,128,512]{2,1,0:T(8,128)(2,1)} %get-tuple-element.18), channel_id=1, source_target_pairs={{0,14},{1,15},{2,0},{3,1},{4,2},{5,3},{6,4},{7,5},{8,6},{9,7},{10,... | collective-permute-start | bytes 786440 | tf_op jit(solution)/shard_map/ppermute | solution.py:179
  56.1 0.7 %copy-start.2 = (f32[128]{0:T(128)S(1)}, f32[128]{0:T(128)}, u32[]{:S(2)}) copy-start(f32[128]{0:T(128)} %param.12) | copy-start | bytes 1540
  56.1 0.7 %copy-start.3 = (f32[128]{0:T(128)S(1)}, f32[128]{0:T(128)}, u32[]{:S(2)}) copy-start(f32[128]{0:T(128)} %param.13) | copy-start | bytes 1540
  56.7 0.9 %copy-start.1 = (bf16[2,128,512]{2,1,0:T(8,128)(2,1)S(1)}, bf16[2,128,512]{2,1,0:T(8,128)(2,1)}, u32[]{:S(2)}) copy-start(bf16[2,128,512]{2,1,0:T(8,128)(2,1)} %get-tuple-element.16.own_ref) | copy-start | bytes 786436

commit v2 on v1

v2 whole, which is shorter than its diff:
```python
import functools
import math

import jax
import jax.numpy as jnp
from jax import lax
from jax.experimental import pallas as pl
from jax.experimental.pallas import tpu as pltpu
from jax.sharding import Mesh, PartitionSpec as P

EPS = 1e-06
LOG2E = math.log2(math.e)
ROWS = (((0,), (0,)), ((), ()))
LAST = (((1,), (1,)), ((), ()))
MIB = 2**20


def rms_parts(x):
    inverse = lax.rsqrt(jnp.mean(x * x, -1, keepdims=True) + EPS)
    return x * inverse, inverse


def token_setup(axis, seg_ref, lag_ref, tok):
    rank = lax.axis_index(axis)

    def seg_block(back):
        start = pl.multiple_of(jnp.maximum(rank - back, 0) * tok, tok)
        row = jnp.broadcast_to(seg_ref[0, :, pl.ds(start, tok)], (tok, tok))
        return jnp.where(rank >= back, row, -1)

    seg_q = seg_block(0).T
    late = jnp.zeros((tok, tok), jnp.int32)
    for r in range(lag_ref.shape[2]):
        late = jnp.where(seg_q == r, lag_ref[0, 0, r], late)
    return seg_q, seg_block, 8.0 / (8.0 + late.astype(jnp.float32))


def stack(ref, heads, group, width):
    first = group * heads
    return jnp.concatenate(
        [
            ref[:, h * width : (h + 1) * width].astype(jnp.float32)
            for h in range(first, first + heads)
        ],
        0,
    )


def spread(tile, heads):
    return jnp.concatenate([tile] * heads, 0)


def query_scale(qg_ref):
    return qg_ref[...] * (qg_ref.shape[1] ** (-0.5) * LOG2E)


def own_kernel(
    axis, q_ref, g_ref, own_ref, seg_ref, lag_ref, qg_ref, kg_ref, p_ref, o_ref, dp_ref,
    halo_bias, coef, bias,
):
    tok, wide = q_ref.shape
    heads = wide // qg_ref.shape[1]

    @pl.when(pl.program_id(0) == 0)
    def _():
        seg_q, seg_block, weight = token_setup(axis, seg_ref, lag_ref, tok)
        row = lax.broadcasted_iota(jnp.int32, (tok, tok), 0)
        col = lax.broadcasted_iota(jnp.int32, (tok, tok), 1)
        bias[...] = jnp.where((seg_block(0) == seg_q) & (col <= row), 0.0, -1e30)
        coef[...] = weight
        halo_bias[:, 0:tok] = jnp.where(seg_block(1) == seg_q, 0.0, -1e30)
        halo_bias[:, tok : 2 * tok] = jnp.where(seg_block(2) == seg_q, 0.0, -1e30)

    qhat, _ = rms_parts(stack(q_ref, heads, 0, kg_ref.shape[1]))
    qs = (qhat * query_scale(qg_ref)).astype(jnp.bfloat16)
    khat, _ = rms_parts(own_ref[0].astype(jnp.float32))
    kn = (khat * kg_ref[...]).astype(jnp.bfloat16)
    v = own_ref[1]
    s = lax.dot_general(qs, kn, LAST, preferred_element_type=jnp.float32)
    p = jnp.exp2(s + spread(bias[...], heads)).astype(jnp.bfloat16)
    p_ref[...] = p
    o_ref[...] = jnp.dot(p, v, preferred_element_type=jnp.float32)
    grad = (stack(g_ref, heads, 0, kg_ref.shape[1]) * spread(coef[...], heads)).astype(jnp.bfloat16)
    dp_ref[...] = lax.dot_general(
        grad, v, LAST, preferred_element_type=jnp.float32
    ).astype(jnp.bfloat16)


def attention_kernel(
    q_ref, g_ref, p_ref, o_ref, dp_ref, bias, coef, own_ref, one_ref, two_ref, qg_ref, kg_ref,
    out_ref, dq_ref, d_own_ref, d_one_ref, d_two_ref, gain_ref, out_buf, dq_buf, sems,
):
    tok, wide = q_ref.shape
    width = qg_ref.shape[1]
    kv_heads = own_ref.shape[2] // width
    part = wide // kv_heads
    heads = part // width
    scale = width ** (-0.5)
    q_gain = qg_ref[...]
    gain = jnp.zeros_like(gain_ref)
    copies = []
    for g in range(kv_heads):
        at_kv = slice(g * width, (g + 1) * width)
        stacked = slice(g * heads * tok, (g + 1) * heads * tok)
        qhat, qr = rms_parts(stack(q_ref, heads, g, width))
        qs = (qhat * query_scale(qg_ref)).astype(jnp.bfloat16)
        refs = (own_ref, one_ref, two_ref)
        khat, _ = rms_parts(
            jnp.concatenate([ref[0, :, at_kv].astype(jnp.float32) for ref in refs], 0)
        )
        kn = (khat * kg_ref[...]).astype(jnp.bfloat16)
        v_halo = jnp.concatenate([ref[1, :, at_kv] for ref in refs[1:]], 0)
        s = lax.dot_general(qs, kn[tok:], LAST, preferred_element_type=jnp.float32)
        p = jnp.exp2(s + spread(bias[...], heads))
        pb = p.astype(jnp.bfloat16)
        p_own = p_ref[stacked, :].astype(jnp.float32)
        inv = 1.0 / jnp.sum(p_own + p[:, :tok] + p[:, tok:], -1, keepdims=True)
        halo = jnp.dot(pb, v_halo, preferred_element_type=jnp.float32)
        out = (o_ref[stacked, :] + halo) * inv
        grad = stack(g_ref, heads, g, width) * spread(coef[...], heads) * inv
        gb = grad.astype(jnp.bfloat16)
        delta = jnp.sum(grad * out, -1, keepdims=True)
        dp = lax.dot_general(gb, v_halo, LAST, preferred_element_type=jnp.float32)
        dp_own = dp_ref[stacked, :].astype(jnp.float32)
        ds = jnp.concatenate(
            [
                (p_own * (dp_own * inv - delta)).astype(jnp.bfloat16),
                (p * (dp - delta)).astype(jnp.bfloat16),
            ],
            1,
        )
        dqn = jnp.dot(ds, kn, preferred_element_type=jnp.float32) * scale
        dk = lax.dot_general(ds, qs, ROWS, preferred_element_type=jnp.float32) * (1.0 / LOG2E)
        p_all = jnp.concatenate([p_ref[stacked, :], pb], 1)
        dv = lax.dot_general(gb, p_all, ROWS, preferred_element_type=jnp.float32).T
        gain += jnp.sum(dqn * qhat, 0, keepdims=True)
        up = dqn * q_gain
        dq = qr * (up - qhat * jnp.mean(up * qhat, -1, keepdims=True))
        for h in range(heads):
            at = slice(h * width, (h + 1) * width)
            rows = slice(h * tok, (h + 1) * tok)
            out_buf[g, :, at] = out[rows].astype(jnp.bfloat16)
            dq_buf[g, :, at] = dq[rows].astype(jnp.bfloat16)
        for i, (buf, ref) in enumerate(((out_buf, out_ref), (dq_buf, dq_ref))):
            copy = pltpu.make_async_copy(
                buf.at[g], ref.at[:, pl.ds(g * part, part)], sems.at[g, i]
            )
            copy.start()
            copies.append(copy)
        for i, ref in enumerate((d_own_ref, d_one_ref, d_two_ref)):
            rows = slice(i * tok, (i + 1) * tok)
            ref[0, :, at_kv] = dk[rows].astype(jnp.bfloat16)
            ref[1, :, at_kv] = dv[rows].astype(jnp.bfloat16)
    gain_ref[...] = gain
    for copy in copies:
        copy.wait()


def finish_kernel(
    kv_ref, own_ref, one_ref, two_ref, parts_ref, qg_ref, kg_ref, out_ref, q_gain_ref, k_gain_ref
):
    width = kg_ref.shape[1]
    gain = kg_ref[...]
    total_gain = jnp.sum(parts_ref[...], 0, keepdims=True)
    q_gain_ref[...] = total_gain
    k_gain_ref[...] = total_gain * qg_ref[...] / gain
    for h in range(kv_ref.shape[2] // width):
        at = slice(h * width, (h + 1) * width)

        def total(i):
            return (
                own_ref[i, :, at].astype(jnp.float32)
                + one_ref[i, :, at].astype(jnp.float32)
                + two_ref[i, :, at].astype(jnp.float32)
            )

        khat, kr = rms_parts(kv_ref[0, :, at].astype(jnp.float32))
        up = total(0) * gain
        dk = kr * (up - khat * jnp.mean(up * khat, -1, keepdims=True))
        out_ref[0, :, at] = dk.astype(jnp.bfloat16)
        out_ref[1, :, at] = total(1).astype(jnp.bfloat16)


def attention(query, grad_out, key_value, one, two, segment_ids, lag, q_gain, k_gain):
    tok, wide = query.shape
    width = q_gain.shape[1]
    kv_heads = key_value.shape[2] // width
    part = wide // kv_heads
    stacked = tok * part // width
    q_spec = pl.BlockSpec((tok, part), lambda g: (0, g))
    kv_spec = pl.BlockSpec((2, tok, width), lambda g: (0, 0, g))
    own_spec = pl.BlockSpec((stacked, width), lambda g: (g, 0))
    whole = lambda a: pl.BlockSpec(a.shape, lambda g: (0,) * a.ndim)
    kept = jax.ShapeDtypeStruct(key_value.shape, jnp.bfloat16)
    rows = jax.ShapeDtypeStruct(query.shape, jnp.bfloat16)
    stack_shape = lambda t: jax.ShapeDtypeStruct((kv_heads * stacked, width), t)
    smem = pl.BlockSpec(memory_space=pltpu.SMEM)
    gains = [whole(q_gain), whole(k_gain)]
    mask = lambda n: jax.ShapeDtypeStruct((tok, n * tok), jnp.float32)
    cost = lambda units: pl.CostEstimate(
        flops=2 * units * tok * tok * wide, bytes_accessed=8 * tok * wide,
        transcendentals=2 * tok * tok * wide // width,
    )
    own = pl.pallas_call(
        functools.partial(own_kernel, "sp"),
        grid=(kv_heads,),
        in_specs=[q_spec, q_spec, kv_spec, whole(segment_ids), smem] + gains,
        out_specs=[own_spec] * 3 + [whole(mask(2)), whole(mask(1))],
        out_shape=[
            stack_shape(jnp.bfloat16), stack_shape(jnp.float32), stack_shape(jnp.bfloat16),
            mask(2), mask(1),
        ],
        scratch_shapes=[pltpu.VMEM((tok, tok), jnp.float32)],
        compiler_params=pltpu.CompilerParams(vmem_limit_bytes=24 * MIB),
        cost_estimate=cost(3),
        name="own",
    )(query, grad_out, key_value, segment_ids, lag, q_gain, k_gain)
    vmem = pl.BlockSpec(memory_space=pltpu.VMEM)
    hbm = pl.BlockSpec(memory_space=pl.ANY)
    return pl.pallas_call(
        attention_kernel,
        in_specs=[vmem] * 12,
        out_specs=[hbm, hbm] + [vmem] * 4,
        out_shape=[rows, rows, kept, kept, kept, jax.ShapeDtypeStruct((1, width), jnp.float32)],
        scratch_shapes=[
            pltpu.VMEM((kv_heads, tok, part), jnp.bfloat16),
            pltpu.VMEM((kv_heads, tok, part), jnp.bfloat16),
            pltpu.SemaphoreType.DMA((kv_heads, 2)),
        ],
        compiler_params=pltpu.CompilerParams(vmem_limit_bytes=28 * MIB),
        cost_estimate=cost(15),
        name="attention",
    )(query, grad_out, *own, key_value, one, two, q_gain, k_gain)


def finish(key_value, own, one, two, parts, q_gain, k_gain):
    vector = jax.ShapeDtypeStruct(k_gain.shape, jnp.float32)
    return pl.pallas_call(
        finish_kernel,
        out_shape=[jax.ShapeDtypeStruct(key_value.shape, jnp.bfloat16), vector, vector],
        compiler_params=pltpu.CompilerParams(vmem_limit_bytes=16 * MIB),
        name="finish",
    )(key_value, own, one, two, parts, q_gain, k_gain)


def local(query, key_value, grad_out, segment_ids, lag, q_gain, k_gain):
    shards = lax.axis_size("sp")
    width = q_gain.shape[0]
    q_gain = q_gain.reshape(1, width)
    k_gain = k_gain.reshape(1, width)

    def shift(x, by):
        pairs = {i: i + by for i in range(shards) if 0 <= i + by < shards}
        free = sorted(set(range(shards)) - set(pairs.values()), reverse=True)
        pairs.update(zip(sorted(set(range(shards)) - set(pairs)), free))
        return lax.ppermute(x, "sp", sorted(pairs.items()))

    one = shift(key_value, 1)
    two = shift(key_value, 2)
    out, d_query, d_own, d_one, d_two, gain = attention(
        query, grad_out, key_value, one, two, segment_ids, lag, q_gain, k_gain
    )
    d_one = shift(d_one, -1)
    d_two = shift(d_two, -2)
    gain = gain + lax.ppermute(gain, "core", [(0, 1), (1, 0)])
    chips = ("chip", "sp")
    copies = jnp.broadcast_to(gain, (lax.axis_size(chips), width))
    parts = lax.all_to_all(copies, chips, 0, 0, tiled=True)
    d_key_value, d_q_gain, d_k_gain = finish(
        key_value, d_own, d_one, d_two, parts, q_gain, k_gain
    )
    return out, d_query, d_key_value, d_q_gain.reshape(width), d_k_gain.reshape(width)


def solution(mesh):
    groups, shards = mesh.devices.shape
    mesh = Mesh(mesh.devices.reshape(groups // 2, 2, shards), ("chip", "core", "sp"))
    tokens = P(("chip", "core", "sp"), None)
    pair = P(None, ("chip", "core", "sp"), None)
    group = P(("chip", "core"), None, None)
    return jax.shard_map(
        local,
        mesh=mesh,
        in_specs=(tokens, pair, tokens, group, group, P(), P()),
        out_specs=(tokens, tokens, pair, P(), P()),
        check_vma=False,
    )
```

time: 58.9 us -> 54.4 us (0.924)
  waiting for transfers between devices: 14 us -> 1.86 us
  local copies, waits for them, and re-layouts: 3 us -> 6.15 us
  starting transfers between devices: 8.37 us -> 10.2 us
  Pallas kernels: 9.45 us -> 11.2 us
  blocking collectives: 23.2 us -> 24 us
    ppermute x4, waiting for transfers between devices: 14 us -> 1.86 us  [shift(): return lax.ppermute(x, 'sp', sorted(pairs.items()))]
    unnamed x14 -> x24, local copies, waits for them, and re-layouts: 2.96 us -> 6.11 us
    pallas_call x1 -> x2, Pallas kernels: 8.45 us -> 10.2 us  [the longest x1 6.68 us: attention(): pl.pallas_call(attention_kernel, in_specs=[vmem] * 12, out_specs=[hbm, hb...]
    ppermute x1, starting transfers between devices: 1.55 us -> 3.27 us  [local(): gain = gain + lax.ppermute(gain, 'core', [(0, 1), (1, 0)])]
    all_to_all x1, blocking collectives: 23.2 us -> 24 us  [local(): parts = lax.all_to_all(copies, chips, 0, 0, tiled=True)]
  transfers between devices with their start and end apart: 5 -> 5, of which waited for: 2 -> 1; matrix products, arithmetic and copies ran while one was open for 0% -> 0% of each run, Pallas kernels for 0% -> 7%
where the time goes in v2:
time: 54.4 us; the launch traced here: 54.1 us
  blocking collectives  24 us (44%)
  Pallas kernels  11.2 us (21%)
  starting transfers between devices  10.2 us (19%)
  local copies, waits for them, and re-layouts  6.15 us (11%)
  waiting for transfers between devices  1.86 us (3%)
  between operations  0.71 us (1%)
    all_to_all x1, blocking collectives, local(): parts = lax.all_to_all(copies, chips, 0, 0, tiled=True)  24 us
    ppermute x4, starting transfers between devices, shift(): return lax.ppermute(x, 'sp', sorted(pairs.items()))  6.91 us
    pallas_call x1, Pallas kernels, attention(): pl.pallas_call(attention_kernel, in_specs=[vmem] * 12, out_specs=[hbm, hb...  6.68 us
    unnamed x24, local copies, waits for them, and re-layouts  6.11 us
    pallas_call x1, Pallas kernels, attention(): pl.pallas_call(functools.partial(own_kernel, 'sp'), grid=(kv_heads,), in_...  3.54 us
    ppermute x1, starting transfers between devices, local(): gain = gain + lax.ppermute(gain, 'core', [(0, 1), (1, 0)])  3.27 us
    ppermute x4, waiting for transfers between devices, shift(): return lax.ppermute(x, 'sp', sorted(pairs.items()))  1.86 us
  transfers between devices with their start and end apart: 5, of which 1 were waited for; matrix products, arithmetic and copies ran while one was open for 0% of the time, Pallas kernels for 7%

profile of v2, /device:TPU:1, one launch (start us, length us, event | category | flops | bytes accessed | tf_op | source)
XLA Modules:
  0.0 54.1 jit_solution(7281076428666122778)
XLA Ops:
  0.6 0.0 copy-start.10
  0.6 0.0 copy-start.8
  0.7 3.8 %collective-permute-start.1 = (bf16[2,128,512]{2,1,0:T(8,128)(2,1)}, bf16[2,128,512]{2,1,0:T(8,128)(2,1)S(1)}, u32[]{:S(2)}, u32[]{:S(2)}) collective-permute-start(bf16[2,128,512]{2,1,0:T(8,128)(2,1)} %kv_ref.1), channel_id=1, source_target_pairs={{0,2},{1,3},{2,4},{3,5},{4,6},{5,7},{6,8},{7,9},{8,10},{9,11},{10,... | collective-permute-start | bytes 786440 | tf_op jit(solution)/shard_map/ppermute | solution.py:256
  4.5 0.4 collective-permute-start
  4.9 0.0 copy-start
  4.9 1.0 %copy-done = bf16[2,128,512]{2,1,0:T(8,128)(2,1)S(1)} copy-done((bf16[2,128,512]{2,1,0:T(8,128)(2,1)S(1)}, bf16[2,128,512]{2,1,0:T(8,128)(2,1)}, u32[]{:S(2)}) %copy-start) | copy-done | bytes 262168
  5.9 0.0 copy-start.2
  5.9 1.2 %copy-done.2 = bf16[128,4096]{1,0:T(8,128)(2,1)S(1)} copy-done((bf16[128,4096]{1,0:T(8,128)(2,1)S(1)}, bf16[128,4096]{1,0:T(8,128)(2,1)}, u32[]{:S(2)}) %copy-start.2) | copy-done | bytes 1048600
  7.1 0.0 copy-start.4
  7.1 1.2 %copy-done.4 = bf16[128,4096]{1,0:T(8,128)(2,1)S(1)} copy-done((bf16[128,4096]{1,0:T(8,128)(2,1)S(1)}, bf16[128,4096]{1,0:T(8,128)(2,1)}, u32[]{:S(2)}) %copy-start.4) | copy-done | bytes 1048600
  8.3 0.0 copy-start.6
  8.3 0.7 %copy-done.6 = s32[1,1,2048]{2,1,0:T(1,128)S(1)} copy-done((s32[1,1,2048]{2,1,0:T(1,128)S(1)}, s32[1,1,2048]{2,1,0:T(1,128)}, u32[]{:S(2)}) %copy-start.6) | copy-done | bytes 8216
  9.0 0.0 copy-start.7
  9.0 0.7 %copy-done.7 = f32[128]{0:T(128)S(1)} copy-done((f32[128]{0:T(128)S(1)}, f32[128]{0:T(128)}, u32[]{:S(2)}) %copy-start.7) | copy-done | bytes 536
  9.7 0.0 copy-start.9
  9.7 0.7 %copy-done.9 = f32[128]{0:T(128)S(1)} copy-done((f32[128]{0:T(128)S(1)}, f32[128]{0:T(128)}, u32[]{:S(2)}) %copy-start.9) | copy-done | bytes 536
  10.3 0.0 copy-start.11
  10.3 0.7 %copy-done.11 = s32[1,1,16]{2,1,0:T(1,128)S(1)} copy-done((s32[1,1,16]{2,1,0:T(1,128)S(1)}, s32[1,1,16]{2,1,0:T(1,128)}, u32[]{:S(2)}) %copy-start.11) | copy-done | bytes 88
  11.0 0.0 copy-start.1
  11.0 0.0 copy-start.3
  11.0 0.0 copy-start.5
  11.0 3.5 %own.1 = (bf16[4096,128]{1,0:T(8,128)(2,1)S(1)}, f32[4096,128]{1,0:T(8,128)S(1)}, bf16[4096,128]{1,0:T(8,128)(2,1)S(1)}, f32[128,256]{1,0:T(8,128)S(1)}, f32[128,128]{1,0:T(8,128)S(1)}) custom-call(bf16[128,4096]{1,0:T(8,128)(2,1)S(1)} %copy-done.2, bf16[128,4096]{1,0:T(8,128)(2,1)S(1)} %copy-done.4, bf16[2,128,512]{2,1,0:T(8,128)(2,1)S(1)} %copy-done, ...), custom_call_target="tpu_custom_call" | custom-call | flops 402653184 | bytes 4194304 | tf_op jit(solution)/shard_map/own/pallas_call | solution.py:204
  14.5 0.0 collective-permute-done.1.two_ref
  14.5 1.9 %collective-permute-done.one_ref = bf16[2,128,512]{2,1,0:T(8,128)(2,1)S(1)} collective-permute-done((bf16[2,128,512]{2,1,0:T(8,128)(2,1)}, bf16[2,128,512]{2,1,0:T(8,128)(2,1)S(1)}, u32[]{:S(2)}, u32[]{:S(2)}) %collective-permute-start) | collective-permute-done | bytes 262176 | tf_op jit(solution)/shard_map/ppermute | solution.py:256
  16.4 0.0 copy-done.10
  16.4 0.0 copy-done.8
  16.4 0.0 copy-done.1
  16.4 0.0 copy-done.3
  16.4 0.0 copy-done.5
  16.4 6.7 %attention.1 = (bf16[128,4096]{1,0:T(8,128)(2,1)}, bf16[128,4096]{1,0:T(8,128)(2,1)}, bf16[2,128,512]{2,1,0:T(8,128)(2,1)S(1)}, bf16[2,128,512]{2,1,0:T(8,128)(2...) custom-call(bf16[128,4096]{1,0:T(8,128)(2,1)S(1)} %copy-done.3, bf16[128,4096]{1,0:T(8,128)(2,1)S(1)} %copy-done.5, ...), custom_call_target="tpu_custom_call" | custom-call | flops 2013265920 | bytes 4194304 | tf_op jit(solution)/shard_map/attention/pallas_call | solution.py:220
  23.1 3.3 %collective-permute-start.4 = (f32[1,128]{1,0:T(1,128)S(1)}, f32[1,128]{1,0:T(1,128)S(1)}, u32[]{:S(2)}, u32[]{:S(2)}) collective-permute-start(f32[1,128]{1,0:T(1,128)S(1)} %get-tuple-element.29), channel_id=1, source_target_pairs={{0,16},{16,0},{1,17},{17,1},{2,18},{18,2},{3,19},{19,3},{4,20},{20... | collective-permute-start | bytes 1544 | tf_op jit(solution)/shard_map/ppermute | solution.py:265
  26.4 1.4 %collective-permute-start.2 = (bf16[2,128,512]{2,1,0:T(8,128)(2,1)S(1)}, bf16[2,128,512]{2,1,0:T(8,128)(2,1)S(1)}, u32[]{:S(2)}, u32[]{:S(2)}) collective-permute-start(bf16[2,128,512]{2,1,0:T(8,128)(2,1)S(1)} %get-tuple-element.27), channel_id=1, source_target_pairs={{0,15},{1,0},{2,1},{3,2},{4,3},{5,4},{6,5},{7,6},{8,7},{9,8},{10,9... | collective-permute-start | bytes 786440 | tf_op jit(solution)/shard_map/ppermute | solution.py:256
  27.8 1.3 %collective-permute-start.3 = (bf16[2,128,512]{2,1,0:T(8,128)(2,1)S(1)}, bf16[2,128,512]{2,1,0:T(8,128)(2,1)S(1)}, u32[]{:S(2)}, u32[]{:S(2)}) collective-permute-start(bf16[2,128,512]{2,1,0:T(8,128)(2,1)S(1)} %get-tuple-element.28), channel_id=1, source_target_pairs={{0,15},{1,14},{2,0},{3,1},{4,2},{5,3},{6,4},{7,5},{8,6},{9,7},{10,... | collective-permute-start | bytes 786440 | tf_op jit(solution)/shard_map/ppermute | solution.py:256
  29.1 0.0 collective-permute-done.4
  29.1 24.0 %all_to_all.8 = f32[128,1,128]{2,1,0:T(1,128)S(1)} all-to-all(f32[128,1,128]{2,1,0:T(1,128)S(1)} %broadcast_in_dim.2), channel_id=1, replica_groups=mesh['chip'=8,'core'=2,'sp'=16] {'chip','sp'}, dimensions={0} | all-to-all | bytes 131072 | tf_op jit(solution)/shard_map/all_to_all | solution.py:268
  53.1 0.0 collective-permute-done.2.one_ref
  53.1 0.0 collective-permute-done.3.two_ref
  53.1 1.0 %finish.1 = (bf16[2,128,512]{2,1,0:T(8,128)(2,1)}, f32[1,128]{1,0:T(1,128)}, f32[1,128]{1,0:T(1,128)}) custom-call(bf16[2,128,512]{2,1,0:T(8,128)(2,1)S(1)} %copy-done.1, bf16[2,128,512]{2,1,0:T(8,128)(2,1)S(1)} %get-tuple-element.26.own_ref, bf16[2,128,512]{2,1,0:T(8,128)(2,1)S(1)} %collective-permute-done.2.one_ref, ...), custom_call_target="tpu_custom_call" | custom-call | tf_op jit(solution)/shard_map/finish/pallas_call | solution.py:238
  (2 shorter events, 0.0 us)
Async XLA Ops:
  0.6 15.8 %copy-start.10 = (f32[128]{0:T(128)S(1)}, f32[128]{0:T(128)}, u32[]{:S(2)}) copy-start(f32[128]{0:T(128)} %param.13) | copy-start | bytes 1540
  0.6 15.8 %copy-start.8 = (f32[128]{0:T(128)S(1)}, f32[128]{0:T(128)}, u32[]{:S(2)}) copy-start(f32[128]{0:T(128)} %param.12) | copy-start | bytes 1540
  0.7 13.9 %collective-permute-start.1 = (bf16[2,128,512]{2,1,0:T(8,128)(2,1)}, bf16[2,128,512]{2,1,0:T(8,128)(2,1)S(1)}, u32[]{:S(2)}, u32[]{:S(2)}) collective-permute-start(bf16[2,128,512]{2,1,0:T(8,128)(2,1)} %kv_ref.1), channel_id=1, source_target_pairs={{0,2},{1,3},{2,4},{3,5},{4,6},{5,7},{6,8},{7,9},{8,10},{9,11},{10,... | collective-permute-start | bytes 786440 | tf_op jit(solution)/shard_map/ppermute | solution.py:256
  4.5 11.9 %collective-permute-start = (bf16[2,128,512]{2,1,0:T(8,128)(2,1)}, bf16[2,128,512]{2,1,0:T(8,128)(2,1)S(1)}, u32[]{:S(2)}, u32[]{:S(2)}) collective-permute-start(bf16[2,128,512]{2,1,0:T(8,128)(2,1)} %kv_ref.1), channel_id=1, source_target_pairs={{0,1},{1,2},{2,3},{3,4},{4,5},{5,6},{6,7},{7,8},{8,9},{9,10},{10,1... | collective-permute-start | bytes 786440 | tf_op jit(solution)/shard_map/ppermute | solution.py:256
  4.9 1.0 %copy-start = (bf16[2,128,512]{2,1,0:T(8,128)(2,1)S(1)}, bf16[2,128,512]{2,1,0:T(8,128)(2,1)}, u32[]{:S(2)}) copy-start(bf16[2,128,512]{2,1,0:T(8,128)(2,1)} %kv_ref.1) | copy-start | bytes 786436
  5.9 1.2 %copy-start.2 = (bf16[128,4096]{1,0:T(8,128)(2,1)S(1)}, bf16[128,4096]{1,0:T(8,128)(2,1)}, u32[]{:S(2)}) copy-start(bf16[128,4096]{1,0:T(8,128)(2,1)} %q_ref.3) | copy-start | bytes 3145732
  7.1 1.2 %copy-start.4 = (bf16[128,4096]{1,0:T(8,128)(2,1)S(1)}, bf16[128,4096]{1,0:T(8,128)(2,1)}, u32[]{:S(2)}) copy-start(bf16[128,4096]{1,0:T(8,128)(2,1)} %g_ref.3) | copy-start | bytes 3145732
  8.3 0.7 %copy-start.6 = (s32[1,1,2048]{2,1,0:T(1,128)S(1)}, s32[1,1,2048]{2,1,0:T(1,128)}, u32[]{:S(2)}) copy-start(s32[1,1,2048]{2,1,0:T(1,128)} %seg_ref.1) | copy-start | bytes 24580
  9.0 0.7 %copy-start.7 = (f32[128]{0:T(128)S(1)}, f32[128]{0:T(128)}, u32[]{:S(2)}) copy-start(f32[128]{0:T(128)} %param.12) | copy-start | bytes 1540
  9.7 0.7 %copy-start.9 = (f32[128]{0:T(128)S(1)}, f32[128]{0:T(128)}, u32[]{:S(2)}) copy-start(f32[128]{0:T(128)} %param.13) | copy-start | bytes 1540
  10.3 0.7 %copy-start.11 = (s32[1,1,16]{2,1,0:T(1,128)S(1)}, s32[1,1,16]{2,1,0:T(1,128)}, u32[]{:S(2)}) copy-start(s32[1,1,16]{2,1,0:T(1,128)} %lag_ref.1) | copy-start | bytes 196
  11.0 5.4 %copy-start.1 = (bf16[2,128,512]{2,1,0:T(8,128)(2,1)S(1)}, bf16[2,128,512]{2,1,0:T(8,128)(2,1)}, u32[]{:S(2)}) copy-start(bf16[2,128,512]{2,1,0:T(8,128)(2,1)} %kv_ref.1) | copy-start | bytes 786436
  11.0 5.4 %copy-start.3 = (bf16[128,4096]{1,0:T(8,128)(2,1)S(1)}, bf16[128,4096]{1,0:T(8,128)(2,1)}, u32[]{:S(2)}) copy-start(bf16[128,4096]{1,0:T(8,128)(2,1)} %q_ref.3) | copy-start | bytes 3145732
  11.0 5.4 %copy-start.5 = (bf16[128,4096]{1,0:T(8,128)(2,1)S(1)}, bf16[128,4096]{1,0:T(8,128)(2,1)}, u32[]{:S(2)}) copy-start(bf16[128,4096]{1,0:T(8,128)(2,1)} %g_ref.3) | copy-start | bytes 3145732
  23.1 6.0 %collective-permute-start.4 = (f32[1,128]{1,0:T(1,128)S(1)}, f32[1,128]{1,0:T(1,128)S(1)}, u32[]{:S(2)}, u32[]{:S(2)}) collective-permute-start(f32[1,128]{1,0:T(1,128)S(1)} %get-tuple-element.29), channel_id=1, source_target_pairs={{0,16},{16,0},{1,17},{17,1},{2,18},{18,2},{3,19},{19,3},{4,20},{20... | collective-permute-start | bytes 1544 | tf_op jit(solution)/shard_map/ppermute | solution.py:265
  26.4 26.7 %collective-permute-start.2 = (bf16[2,128,512]{2,1,0:T(8,128)(2,1)S(1)}, bf16[2,128,512]{2,1,0:T(8,128)(2,1)S(1)}, u32[]{:S(2)}, u32[]{:S(2)}) collective-permute-start(bf16[2,128,512]{2,1,0:T(8,128)(2,1)S(1)} %get-tuple-element.27), channel_id=1, source_target_pairs={{0,15},{1,0},{2,1},{3,2},{4,3},{5,4},{6,5},{7,6},{8,7},{9,8},{10,9... | collective-permute-start | bytes 786440 | tf_op jit(solution)/shard_map/ppermute | solution.py:256
  27.8 25.3 %collective-permute-start.3 = (bf16[2,128,512]{2,1,0:T(8,128)(2,1)S(1)}, bf16[2,128,512]{2,1,0:T(8,128)(2,1)S(1)}, u32[]{:S(2)}, u32[]{:S(2)}) collective-permute-start(bf16[2,128,512]{2,1,0:T(8,128)(2,1)S(1)} %get-tuple-element.28), channel_id=1, source_target_pairs={{0,15},{1,14},{2,0},{3,1},{4,2},{5,3},{6,4},{7,5},{8,6},{9,7},{10,... | collective-permute-start | bytes 786440 | tf_op jit(solution)/shard_map/ppermute | solution.py:256

commit v3 on v2

--- a/solution.py
+++ b/solution.py
@@ -97,9 +97,10 @@
     heads = part // width
     scale = width ** (-0.5)
     q_gain = qg_ref[...]
-    gain = jnp.zeros_like(gain_ref)
     copies = []
-    for g in range(kv_heads):
+    gains = []
+
+    def scores(g):
         at_kv = slice(g * width, (g + 1) * width)
         stacked = slice(g * heads * tok, (g + 1) * heads * tok)
         qhat, qr = rms_parts(stack(q_ref, heads, g, width))
@@ -109,18 +110,24 @@
             jnp.concatenate([ref[0, :, at_kv].astype(jnp.float32) for ref in refs], 0)
         )
         kn = (khat * kg_ref[...]).astype(jnp.bfloat16)
-        v_halo = jnp.concatenate([ref[1, :, at_kv] for ref in refs[1:]], 0)
         s = lax.dot_general(qs, kn[tok:], LAST, preferred_element_type=jnp.float32)
         p = jnp.exp2(s + spread(bias[...], heads))
         pb = p.astype(jnp.bfloat16)
         p_own = p_ref[stacked, :].astype(jnp.float32)
         inv = 1.0 / jnp.sum(p_own + p[:, :tok] + p[:, tok:], -1, keepdims=True)
+        return g, qhat, qr, qs, kn, p, pb, inv
+
+    def weights(g, qhat, qr, qs, kn, p, pb, inv):
+        at_kv = slice(g * width, (g + 1) * width)
+        stacked = slice(g * heads * tok, (g + 1) * heads * tok)
+        v_halo = jnp.concatenate([ref[1, :, at_kv] for ref in (one_ref, two_ref)], 0)
         halo = jnp.dot(pb, v_halo, preferred_element_type=jnp.float32)
         out = (o_ref[stacked, :] + halo) * inv
         grad = stack(g_ref, heads, g, width) * spread(coef[...], heads) * inv
         gb = grad.astype(jnp.bfloat16)
         delta = jnp.sum(grad * out, -1, keepdims=True)
         dp = lax.dot_general(gb, v_halo, LAST, preferred_element_type=jnp.float32)
+        p_own = p_ref[stacked, :].astype(jnp.float32)
         dp_own = dp_ref[stacked, :].astype(jnp.float32)
         ds = jnp.concatenate(
             [
@@ -129,18 +136,24 @@
             ],
             1,
         )
+        for h in range(heads):
+            rows = slice(h * tok, (h + 1) * tok)
+            out_buf[g, :, h * width : (h + 1) * width] = out[rows].astype(jnp.bfloat16)
+        return g, qhat, qr, qs, kn, pb, gb, ds
+
+    def gradients(g, qhat, qr, qs, kn, pb, gb, ds):
+        at_kv = slice(g * width, (g + 1) * width)
+        stacked = slice(g * heads * tok, (g + 1) * heads * tok)
         dqn = jnp.dot(ds, kn, preferred_element_type=jnp.float32) * scale
-        dk = lax.dot_general(ds, qs, ROWS, preferred_element_type=jnp.float32) * (1.0 / LOG2E)
+        dk = lax.dot_general(qs, ds, ROWS, preferred_element_type=jnp.float32).T * (1.0 / LOG2E)
         p_all = jnp.concatenate([p_ref[stacked, :], pb], 1)
         dv = lax.dot_general(gb, p_all, ROWS, preferred_element_type=jnp.float32).T
-        gain += jnp.sum(dqn * qhat, 0, keepdims=True)
+        gains.append(jnp.sum(dqn * qhat, 0, keepdims=True))
         up = dqn * q_gain
         dq = qr * (up - qhat * jnp.mean(up * qhat, -1, keepdims=True))
         for h in range(heads):
-            at = slice(h * width, (h + 1) * width)
             rows = slice(h * tok, (h + 1) * tok)
-            out_buf[g, :, at] = out[rows].astype(jnp.bfloat16)
-            dq_buf[g, :, at] = dq[rows].astype(jnp.bfloat16)
+            dq_buf[g, :, h * width : (h + 1) * width] = dq[rows].astype(jnp.bfloat16)
         for i, (buf, ref) in enumerate(((out_buf, out_ref), (dq_buf, dq_ref))):
             copy = pltpu.make_async_copy(
                 buf.at[g], ref.at[:, pl.ds(g * part, part)], sems.at[g, i]
@@ -151,6 +164,16 @@
             rows = slice(i * tok, (i + 1) * tok)
             ref[0, :, at_kv] = dk[rows].astype(jnp.bfloat16)
             ref[1, :, at_kv] = dv[rows].astype(jnp.bfloat16)
+
+    first, second = {}, {}
+    for t in range(kv_heads + 2):
+        if t - 2 in second:
+            gradients(*second[t - 2])
+        if t - 1 in first:
+            second[t - 1] = weights(*first[t - 1])
+        if t < kv_heads:
+            first[t] = scores(t)
+    gain = sum(gains[1:], gains[0])
     gain_ref[...] = gain
     for copy in copies:
         copy.wait()
@@ -267,7 +290,7 @@
     copies = jnp.broadcast_to(gain, (lax.axis_size(chips), width))
     parts = lax.all_to_all(copies, chips, 0, 0, tiled=True)
     d_key_value, d_q_gain, d_k_gain = finish(
-        key_value, d_own, d_one, d_two, parts, q_gain, k_gain
+        key_value, d_own, d_two, d_one, parts, q_gain, k_gain
     )
     return out, d_query, d_key_value, d_q_gain.reshape(width), d_k_gain.reshape(width)
 

time: 54.4 us -> 53.5 us (0.983)
  blocking collectives: 24 us -> 22 us
  starting transfers between devices: 10.2 us -> 11.6 us
    all_to_all x1, blocking collectives: 24 us -> 22 us  [local(): parts = lax.all_to_all(copies, chips, 0, 0, tiled=True)]
    ppermute x4, starting transfers between devices: 6.91 us -> 8.31 us  [shift(): return lax.ppermute(x, 'sp', sorted(pairs.items()))]
where the time goes in v3:
time: 53.5 us; the launch traced here: 53.2 us
  blocking collectives  22 us (41%)
  starting transfers between devices  11.6 us (22%)
  Pallas kernels  10.9 us (20%)
  local copies, waits for them, and re-layouts  6.15 us (11%)
  waiting for transfers between devices  1.86 us (3%)
  between operations  0.71 us (1%)
    all_to_all x1, blocking collectives, local(): parts = lax.all_to_all(copies, chips, 0, 0, tiled=True)  22 us
    ppermute x4, starting transfers between devices, shift(): return lax.ppermute(x, 'sp', sorted(pairs.items()))  8.31 us
    pallas_call x1, Pallas kernels, attention(): pl.pallas_call(attention_kernel, in_specs=[vmem] * 12, out_specs=[hbm, hb...  6.4 us
    unnamed x24, local copies, waits for them, and re-layouts  6.11 us
    pallas_call x1, Pallas kernels, attention(): pl.pallas_call(functools.partial(own_kernel, 'sp'), grid=(kv_heads,), in_...  3.54 us
    ppermute x1, starting transfers between devices, local(): gain = gain + lax.ppermute(gain, 'core', [(0, 1), (1, 0)])  3.27 us
    ppermute x4, waiting for transfers between devices, shift(): return lax.ppermute(x, 'sp', sorted(pairs.items()))  1.86 us
  transfers between devices with their start and end apart: 5, of which 1 were waited for; matrix products, arithmetic and copies ran while one was open for 0% of the time, Pallas kernels for 7%

profile of v3, /device:TPU:1, one launch (start us, length us, event | category | flops | bytes accessed | tf_op | source)
XLA Modules:
  0.0 53.2 jit_solution(1653059226529173875)
XLA Ops:
  0.6 0.0 copy-start.10
  0.6 0.0 copy-start.8
  0.7 3.8 %collective-permute-start.1 = (bf16[2,128,512]{2,1,0:T(8,128)(2,1)}, bf16[2,128,512]{2,1,0:T(8,128)(2,1)S(1)}, u32[]{:S(2)}, u32[]{:S(2)}) collective-permute-start(bf16[2,128,512]{2,1,0:T(8,128)(2,1)} %kv_ref.1), channel_id=1, source_target_pairs={{0,2},{1,3},{2,4},{3,5},{4,6},{5,7},{6,8},{7,9},{8,10},{9,11},{10,... | collective-permute-start | bytes 786440 | tf_op jit(solution)/shard_map/ppermute | solution.py:279
  4.5 0.4 collective-permute-start
  4.9 0.0 copy-start
  4.9 1.0 %copy-done = bf16[2,128,512]{2,1,0:T(8,128)(2,1)S(1)} copy-done((bf16[2,128,512]{2,1,0:T(8,128)(2,1)S(1)}, bf16[2,128,512]{2,1,0:T(8,128)(2,1)}, u32[]{:S(2)}) %copy-start) | copy-done | bytes 262168
  5.9 0.0 copy-start.2
  5.9 1.2 %copy-done.2 = bf16[128,4096]{1,0:T(8,128)(2,1)S(1)} copy-done((bf16[128,4096]{1,0:T(8,128)(2,1)S(1)}, bf16[128,4096]{1,0:T(8,128)(2,1)}, u32[]{:S(2)}) %copy-start.2) | copy-done | bytes 1048600
  7.1 0.0 copy-start.4
  7.1 1.2 %copy-done.4 = bf16[128,4096]{1,0:T(8,128)(2,1)S(1)} copy-done((bf16[128,4096]{1,0:T(8,128)(2,1)S(1)}, bf16[128,4096]{1,0:T(8,128)(2,1)}, u32[]{:S(2)}) %copy-start.4) | copy-done | bytes 1048600
  8.3 0.0 copy-start.6
  8.3 0.7 %copy-done.6 = s32[1,1,2048]{2,1,0:T(1,128)S(1)} copy-done((s32[1,1,2048]{2,1,0:T(1,128)S(1)}, s32[1,1,2048]{2,1,0:T(1,128)}, u32[]{:S(2)}) %copy-start.6) | copy-done | bytes 8216
  9.0 0.0 copy-start.7
  9.0 0.7 %copy-done.7 = f32[128]{0:T(128)S(1)} copy-done((f32[128]{0:T(128)S(1)}, f32[128]{0:T(128)}, u32[]{:S(2)}) %copy-start.7) | copy-done | bytes 536
  9.7 0.0 copy-start.9
  9.7 0.7 %copy-done.9 = f32[128]{0:T(128)S(1)} copy-done((f32[128]{0:T(128)S(1)}, f32[128]{0:T(128)}, u32[]{:S(2)}) %copy-start.9) | copy-done | bytes 536
  10.3 0.0 copy-start.11
  10.3 0.7 %copy-done.11 = s32[1,1,16]{2,1,0:T(1,128)S(1)} copy-done((s32[1,1,16]{2,1,0:T(1,128)S(1)}, s32[1,1,16]{2,1,0:T(1,128)}, u32[]{:S(2)}) %copy-start.11) | copy-done | bytes 88
  11.0 0.0 copy-start.1
  11.0 0.0 copy-start.3
  11.0 0.0 copy-start.5
  11.0 3.5 %own.1 = (bf16[4096,128]{1,0:T(8,128)(2,1)S(1)}, f32[4096,128]{1,0:T(8,128)S(1)}, bf16[4096,128]{1,0:T(8,128)(2,1)S(1)}, f32[128,256]{1,0:T(8,128)S(1)}, f32[128,128]{1,0:T(8,128)S(1)}) custom-call(bf16[128,4096]{1,0:T(8,128)(2,1)S(1)} %copy-done.2, bf16[128,4096]{1,0:T(8,128)(2,1)S(1)} %copy-done.4, bf16[2,128,512]{2,1,0:T(8,128)(2,1)S(1)} %copy-done, ...), custom_call_target="tpu_custom_call" | custom-call | flops 402653184 | bytes 4194304 | tf_op jit(solution)/shard_map/own/pallas_call | solution.py:227
  14.5 0.0 collective-permute-done.1.two_ref
  14.5 1.9 %collective-permute-done.one_ref = bf16[2,128,512]{2,1,0:T(8,128)(2,1)S(1)} collective-permute-done((bf16[2,128,512]{2,1,0:T(8,128)(2,1)}, bf16[2,128,512]{2,1,0:T(8,128)(2,1)S(1)}, u32[]{:S(2)}, u32[]{:S(2)}) %collective-permute-start) | collective-permute-done | bytes 262176 | tf_op jit(solution)/shard_map/ppermute | solution.py:279
  16.4 0.0 copy-done.10
  16.4 0.0 copy-done.8
  16.4 0.0 copy-done.1
  16.4 0.0 copy-done.3
  16.4 0.0 copy-done.5
  16.4 6.4 %attention.1 = (bf16[128,4096]{1,0:T(8,128)(2,1)}, bf16[128,4096]{1,0:T(8,128)(2,1)}, bf16[2,128,512]{2,1,0:T(8,128)(2,1)S(1)}, bf16[2,128,512]{2,1,0:T(8,128)(2...) custom-call(bf16[128,4096]{1,0:T(8,128)(2,1)S(1)} %copy-done.3, bf16[128,4096]{1,0:T(8,128)(2,1)S(1)} %copy-done.5, ...), custom_call_target="tpu_custom_call" | custom-call | flops 2013265920 | bytes 4194304 | tf_op jit(solution)/shard_map/attention/pallas_call | solution.py:243
  22.8 3.3 %collective-permute-start.4 = (f32[1,128]{1,0:T(1,128)S(1)}, f32[1,128]{1,0:T(1,128)S(1)}, u32[]{:S(2)}, u32[]{:S(2)}) collective-permute-start(f32[1,128]{1,0:T(1,128)S(1)} %get-tuple-element.29), channel_id=1, source_target_pairs={{0,16},{16,0},{1,17},{17,1},{2,18},{18,2},{3,19},{19,3},{4,20},{20... | collective-permute-start | bytes 1544 | tf_op jit(solution)/shard_map/ppermute | solution.py:288
  26.1 1.4 %collective-permute-start.2 = (bf16[2,128,512]{2,1,0:T(8,128)(2,1)S(1)}, bf16[2,128,512]{2,1,0:T(8,128)(2,1)S(1)}, u32[]{:S(2)}, u32[]{:S(2)}) collective-permute-start(bf16[2,128,512]{2,1,0:T(8,128)(2,1)S(1)} %get-tuple-element.27), channel_id=1, source_target_pairs={{0,15},{1,14},{2,0},{3,1},{4,2},{5,3},{6,4},{7,5},{8,6},{9,7},{10,... | collective-permute-start | bytes 786440 | tf_op jit(solution)/shard_map/ppermute | solution.py:279
  27.5 2.7 %collective-permute-start.3 = (bf16[2,128,512]{2,1,0:T(8,128)(2,1)S(1)}, bf16[2,128,512]{2,1,0:T(8,128)(2,1)S(1)}, u32[]{:S(2)}, u32[]{:S(2)}) collective-permute-start(bf16[2,128,512]{2,1,0:T(8,128)(2,1)S(1)} %get-tuple-element.28), channel_id=1, source_target_pairs={{0,15},{1,0},{2,1},{3,2},{4,3},{5,4},{6,5},{7,6},{8,7},{9,8},{10,9... | collective-permute-start | bytes 786440 | tf_op jit(solution)/shard_map/ppermute | solution.py:279
  30.2 0.0 collective-permute-done.4
  30.2 22.0 %all_to_all.8 = f32[128,1,128]{2,1,0:T(1,128)S(1)} all-to-all(f32[128,1,128]{2,1,0:T(1,128)S(1)} %broadcast_in_dim.2), channel_id=1, replica_groups=mesh['chip'=8,'core'=2,'sp'=16] {'chip','sp'}, dimensions={0} | all-to-all | bytes 131072 | tf_op jit(solution)/shard_map/all_to_all | solution.py:291
  52.2 0.0 collective-permute-done.2.one_ref
  52.2 0.0 collective-permute-done.3.two_ref
  52.2 1.0 %finish.1 = (bf16[2,128,512]{2,1,0:T(8,128)(2,1)}, f32[1,128]{1,0:T(1,128)}, f32[1,128]{1,0:T(1,128)}) custom-call(bf16[2,128,512]{2,1,0:T(8,128)(2,1)S(1)} %copy-done.1, bf16[2,128,512]{2,1,0:T(8,128)(2,1)S(1)} %get-tuple-element.26.own_ref, bf16[2,128,512]{2,1,0:T(8,128)(2,1)S(1)} %collective-permute-done.2.one_ref, ...), custom_call_target="tpu_custom_call" | custom-call | tf_op jit(solution)/shard_map/finish/pallas_call | solution.py:261
  (2 shorter events, 0.0 us)
Async XLA Ops:
  0.6 15.8 %copy-start.10 = (f32[128]{0:T(128)S(1)}, f32[128]{0:T(128)}, u32[]{:S(2)}) copy-start(f32[128]{0:T(128)} %param.13) | copy-start | bytes 1540
  0.6 15.8 %copy-start.8 = (f32[128]{0:T(128)S(1)}, f32[128]{0:T(128)}, u32[]{:S(2)}) copy-start(f32[128]{0:T(128)} %param.12) | copy-start | bytes 1540
  0.7 13.9 %collective-permute-start.1 = (bf16[2,128,512]{2,1,0:T(8,128)(2,1)}, bf16[2,128,512]{2,1,0:T(8,128)(2,1)S(1)}, u32[]{:S(2)}, u32[]{:S(2)}) collective-permute-start(bf16[2,128,512]{2,1,0:T(8,128)(2,1)} %kv_ref.1), channel_id=1, source_target_pairs={{0,2},{1,3},{2,4},{3,5},{4,6},{5,7},{6,8},{7,9},{8,10},{9,11},{10,... | collective-permute-start | bytes 786440 | tf_op jit(solution)/shard_map/ppermute | solution.py:279
  4.5 11.9 %collective-permute-start = (bf16[2,128,512]{2,1,0:T(8,128)(2,1)}, bf16[2,128,512]{2,1,0:T(8,128)(2,1)S(1)}, u32[]{:S(2)}, u32[]{:S(2)}) collective-permute-start(bf16[2,128,512]{2,1,0:T(8,128)(2,1)} %kv_ref.1), channel_id=1, source_target_pairs={{0,1},{1,2},{2,3},{3,4},{4,5},{5,6},{6,7},{7,8},{8,9},{9,10},{10,1... | collective-permute-start | bytes 786440 | tf_op jit(solution)/shard_map/ppermute | solution.py:279
  4.9 1.0 %copy-start = (bf16[2,128,512]{2,1,0:T(8,128)(2,1)S(1)}, bf16[2,128,512]{2,1,0:T(8,128)(2,1)}, u32[]{:S(2)}) copy-start(bf16[2,128,512]{2,1,0:T(8,128)(2,1)} %kv_ref.1) | copy-start | bytes 786436
  5.9 1.2 %copy-start.2 = (bf16[128,4096]{1,0:T(8,128)(2,1)S(1)}, bf16[128,4096]{1,0:T(8,128)(2,1)}, u32[]{:S(2)}) copy-start(bf16[128,4096]{1,0:T(8,128)(2,1)} %q_ref.3) | copy-start | bytes 3145732
  7.1 1.2 %copy-start.4 = (bf16[128,4096]{1,0:T(8,128)(2,1)S(1)}, bf16[128,4096]{1,0:T(8,128)(2,1)}, u32[]{:S(2)}) copy-start(bf16[128,4096]{1,0:T(8,128)(2,1)} %g_ref.3) | copy-start | bytes 3145732
  8.3 0.7 %copy-start.6 = (s32[1,1,2048]{2,1,0:T(1,128)S(1)}, s32[1,1,2048]{2,1,0:T(1,128)}, u32[]{:S(2)}) copy-start(s32[1,1,2048]{2,1,0:T(1,128)} %seg_ref.1) | copy-start | bytes 24580
  9.0 0.7 %copy-start.7 = (f32[128]{0:T(128)S(1)}, f32[128]{0:T(128)}, u32[]{:S(2)}) copy-start(f32[128]{0:T(128)} %param.12) | copy-start | bytes 1540
  9.7 0.7 %copy-start.9 = (f32[128]{0:T(128)S(1)}, f32[128]{0:T(128)}, u32[]{:S(2)}) copy-start(f32[128]{0:T(128)} %param.13) | copy-start | bytes 1540
  10.3 0.7 %copy-start.11 = (s32[1,1,16]{2,1,0:T(1,128)S(1)}, s32[1,1,16]{2,1,0:T(1,128)}, u32[]{:S(2)}) copy-start(s32[1,1,16]{2,1,0:T(1,128)} %lag_ref.1) | copy-start | bytes 196
  11.0 5.4 %copy-start.1 = (bf16[2,128,512]{2,1,0:T(8,128)(2,1)S(1)}, bf16[2,128,512]{2,1,0:T(8,128)(2,1)}, u32[]{:S(2)}) copy-start(bf16[2,128,512]{2,1,0:T(8,128)(2,1)} %kv_ref.1) | copy-start | bytes 786436
  11.0 5.4 %copy-start.3 = (bf16[128,4096]{1,0:T(8,128)(2,1)S(1)}, bf16[128,4096]{1,0:T(8,128)(2,1)}, u32[]{:S(2)}) copy-start(bf16[128,4096]{1,0:T(8,128)(2,1)} %q_ref.3) | copy-start | bytes 3145732
  11.0 5.4 %copy-start.5 = (bf16[128,4096]{1,0:T(8,128)(2,1)S(1)}, bf16[128,4096]{1,0:T(8,128)(2,1)}, u32[]{:S(2)}) copy-start(bf16[128,4096]{1,0:T(8,128)(2,1)} %g_ref.3) | copy-start | bytes 3145732
  22.8 7.4 %collective-permute-start.4 = (f32[1,128]{1,0:T(1,128)S(1)}, f32[1,128]{1,0:T(1,128)S(1)}, u32[]{:S(2)}, u32[]{:S(2)}) collective-permute-start(f32[1,128]{1,0:T(1,128)S(1)} %get-tuple-element.29), channel_id=1, source_target_pairs={{0,16},{16,0},{1,17},{17,1},{2,18},{18,2},{3,19},{19,3},{4,20},{20... | collective-permute-start | bytes 1544 | tf_op jit(solution)/shard_map/ppermute | solution.py:288
  26.1 26.1 %collective-permute-start.2 = (bf16[2,128,512]{2,1,0:T(8,128)(2,1)S(1)}, bf16[2,128,512]{2,1,0:T(8,128)(2,1)S(1)}, u32[]{:S(2)}, u32[]{:S(2)}) collective-permute-start(bf16[2,128,512]{2,1,0:T(8,128)(2,1)S(1)} %get-tuple-element.27), channel_id=1, source_target_pairs={{0,15},{1,14},{2,0},{3,1},{4,2},{5,3},{6,4},{7,5},{8,6},{9,7},{10,... | collective-permute-start | bytes 786440 | tf_op jit(solution)/shard_map/ppermute | solution.py:279
  27.5 24.7 %collective-permute-start.3 = (bf16[2,128,512]{2,1,0:T(8,128)(2,1)S(1)}, bf16[2,128,512]{2,1,0:T(8,128)(2,1)S(1)}, u32[]{:S(2)}, u32[]{:S(2)}) collective-permute-start(bf16[2,128,512]{2,1,0:T(8,128)(2,1)S(1)} %get-tuple-element.28), channel_id=1, source_target_pairs={{0,15},{1,0},{2,1},{3,2},{4,3},{5,4},{6,5},{7,6},{8,7},{9,8},{10,9... | collective-permute-start | bytes 786440 | tf_op jit(solution)/shard_map/ppermute | solution.py:279

commit v4 on v3

--- a/solution.py
+++ b/solution.py
@@ -144,13 +144,13 @@
     def gradients(g, qhat, qr, qs, kn, pb, gb, ds):
         at_kv = slice(g * width, (g + 1) * width)
         stacked = slice(g * heads * tok, (g + 1) * heads * tok)
-        dqn = jnp.dot(ds, kn, preferred_element_type=jnp.float32) * scale
+        up = jnp.dot(ds, kn, preferred_element_type=jnp.float32) * (q_gain * scale)
         dk = lax.dot_general(qs, ds, ROWS, preferred_element_type=jnp.float32).T * (1.0 / LOG2E)
         p_all = jnp.concatenate([p_ref[stacked, :], pb], 1)
         dv = lax.dot_general(gb, p_all, ROWS, preferred_element_type=jnp.float32).T
-        gains.append(jnp.sum(dqn * qhat, 0, keepdims=True))
-        up = dqn * q_gain
-        dq = qr * (up - qhat * jnp.mean(up * qhat, -1, keepdims=True))
+        both = up * qhat
+        gains.append(jnp.sum(both, 0, keepdims=True))
+        dq = qr * (up - qhat * jnp.mean(both, -1, keepdims=True))
         for h in range(heads):
             rows = slice(h * tok, (h + 1) * tok)
             dq_buf[g, :, h * width : (h + 1) * width] = dq[rows].astype(jnp.bfloat16)
@@ -185,8 +185,8 @@
     width = kg_ref.shape[1]
     gain = kg_ref[...]
     total_gain = jnp.sum(parts_ref[...], 0, keepdims=True)
-    q_gain_ref[...] = total_gain
-    k_gain_ref[...] = total_gain * qg_ref[...] / gain
+    q_gain_ref[...] = total_gain / qg_ref[...]
+    k_gain_ref[...] = total_gain / gain
     for h in range(kv_ref.shape[2] // width):
         at = slice(h * width, (h + 1) * width)
 

time: 53.5 us -> 53.4 us (level)
  no operation moved by 1% of the time
where the time goes in v4:
time: 53.4 us; the launch traced here: 53.1 us
  blocking collectives  22 us (41%)
  starting transfers between devices  11.6 us (22%)
  Pallas kernels  10.8 us (20%)
  local copies, waits for them, and re-layouts  6.15 us (12%)
  waiting for transfers between devices  1.86 us (3%)
  between operations  0.71 us (1%)
    all_to_all x1, blocking collectives, local(): parts = lax.all_to_all(copies, chips, 0, 0, tiled=True)  22 us
    ppermute x4, starting transfers between devices, shift(): return lax.ppermute(x, 'sp', sorted(pairs.items()))  8.31 us
    pallas_call x1, Pallas kernels, attention(): pl.pallas_call(attention_kernel, in_specs=[vmem] * 12, out_specs=[hbm, hb...  6.28 us
    unnamed x24, local copies, waits for them, and re-layouts  6.11 us
    pallas_call x1, Pallas kernels, attention(): pl.pallas_call(functools.partial(own_kernel, 'sp'), grid=(kv_heads,), in_...  3.54 us
    ppermute x1, starting transfers between devices, local(): gain = gain + lax.ppermute(gain, 'core', [(0, 1), (1, 0)])  3.27 us
    ppermute x4, waiting for transfers between devices, shift(): return lax.ppermute(x, 'sp', sorted(pairs.items()))  1.86 us
  transfers between devices with their start and end apart: 5, of which 1 were waited for; matrix products, arithmetic and copies ran while one was open for 0% of the time, Pallas kernels for 7%

profile of v4, /device:TPU:1, one launch (start us, length us, event | category | flops | bytes accessed | tf_op | source)
XLA Modules:
  0.0 53.1 jit_solution(11964365879903559766)
XLA Ops:
  0.6 0.0 copy-start.10
  0.6 0.0 copy-start.8
  0.7 3.8 %collective-permute-start.1 = (bf16[2,128,512]{2,1,0:T(8,128)(2,1)}, bf16[2,128,512]{2,1,0:T(8,128)(2,1)S(1)}, u32[]{:S(2)}, u32[]{:S(2)}) collective-permute-start(bf16[2,128,512]{2,1,0:T(8,128)(2,1)} %kv_ref.1), channel_id=1, source_target_pairs={{0,2},{1,3},{2,4},{3,5},{4,6},{5,7},{6,8},{7,9},{8,10},{9,11},{10,... | collective-permute-start | bytes 786440 | tf_op jit(solution)/shard_map/ppermute | solution.py:279
  4.5 0.4 collective-permute-start
  4.9 0.0 copy-start
  4.9 1.0 %copy-done = bf16[2,128,512]{2,1,0:T(8,128)(2,1)S(1)} copy-done((bf16[2,128,512]{2,1,0:T(8,128)(2,1)S(1)}, bf16[2,128,512]{2,1,0:T(8,128)(2,1)}, u32[]{:S(2)}) %copy-start) | copy-done | bytes 262168
  5.9 0.0 copy-start.2
  5.9 1.2 %copy-done.2 = bf16[128,4096]{1,0:T(8,128)(2,1)S(1)} copy-done((bf16[128,4096]{1,0:T(8,128)(2,1)S(1)}, bf16[128,4096]{1,0:T(8,128)(2,1)}, u32[]{:S(2)}) %copy-start.2) | copy-done | bytes 1048600
  7.1 0.0 copy-start.4
  7.1 1.2 %copy-done.4 = bf16[128,4096]{1,0:T(8,128)(2,1)S(1)} copy-done((bf16[128,4096]{1,0:T(8,128)(2,1)S(1)}, bf16[128,4096]{1,0:T(8,128)(2,1)}, u32[]{:S(2)}) %copy-start.4) | copy-done | bytes 1048600
  8.3 0.0 copy-start.6
  8.3 0.7 %copy-done.6 = s32[1,1,2048]{2,1,0:T(1,128)S(1)} copy-done((s32[1,1,2048]{2,1,0:T(1,128)S(1)}, s32[1,1,2048]{2,1,0:T(1,128)}, u32[]{:S(2)}) %copy-start.6) | copy-done | bytes 8216
  9.0 0.0 copy-start.7
  9.0 0.7 %copy-done.7 = f32[128]{0:T(128)S(1)} copy-done((f32[128]{0:T(128)S(1)}, f32[128]{0:T(128)}, u32[]{:S(2)}) %copy-start.7) | copy-done | bytes 536
  9.7 0.0 copy-start.9
  9.7 0.7 %copy-done.9 = f32[128]{0:T(128)S(1)} copy-done((f32[128]{0:T(128)S(1)}, f32[128]{0:T(128)}, u32[]{:S(2)}) %copy-start.9) | copy-done | bytes 536
  10.3 0.0 copy-start.11
  10.3 0.7 %copy-done.11 = s32[1,1,16]{2,1,0:T(1,128)S(1)} copy-done((s32[1,1,16]{2,1,0:T(1,128)S(1)}, s32[1,1,16]{2,1,0:T(1,128)}, u32[]{:S(2)}) %copy-start.11) | copy-done | bytes 88
  11.0 0.0 copy-start.1
  11.0 0.0 copy-start.3
  11.0 0.0 copy-start.5
  11.0 3.5 %own.1 = (bf16[4096,128]{1,0:T(8,128)(2,1)S(1)}, f32[4096,128]{1,0:T(8,128)S(1)}, bf16[4096,128]{1,0:T(8,128)(2,1)S(1)}, f32[128,256]{1,0:T(8,128)S(1)}, f32[128,128]{1,0:T(8,128)S(1)}) custom-call(bf16[128,4096]{1,0:T(8,128)(2,1)S(1)} %copy-done.2, bf16[128,4096]{1,0:T(8,128)(2,1)S(1)} %copy-done.4, bf16[2,128,512]{2,1,0:T(8,128)(2,1)S(1)} %copy-done, ...), custom_call_target="tpu_custom_call" | custom-call | flops 402653184 | bytes 4194304 | tf_op jit(solution)/shard_map/own/pallas_call | solution.py:227
  14.5 0.0 collective-permute-done.1.two_ref
  14.5 1.9 %collective-permute-done.one_ref = bf16[2,128,512]{2,1,0:T(8,128)(2,1)S(1)} collective-permute-done((bf16[2,128,512]{2,1,0:T(8,128)(2,1)}, bf16[2,128,512]{2,1,0:T(8,128)(2,1)S(1)}, u32[]{:S(2)}, u32[]{:S(2)}) %collective-permute-start) | collective-permute-done | bytes 262176 | tf_op jit(solution)/shard_map/ppermute | solution.py:279
  16.4 0.0 copy-done.10
  16.4 0.0 copy-done.8
  16.4 0.0 copy-done.1
  16.4 0.0 copy-done.3
  16.4 0.0 copy-done.5
  16.4 6.3 %attention.1 = (bf16[128,4096]{1,0:T(8,128)(2,1)}, bf16[128,4096]{1,0:T(8,128)(2,1)}, bf16[2,128,512]{2,1,0:T(8,128)(2,1)S(1)}, bf16[2,128,512]{2,1,0:T(8,128)(2...) custom-call(bf16[128,4096]{1,0:T(8,128)(2,1)S(1)} %copy-done.3, bf16[128,4096]{1,0:T(8,128)(2,1)S(1)} %copy-done.5, ...), custom_call_target="tpu_custom_call" | custom-call | flops 2013265920 | bytes 4194304 | tf_op jit(solution)/shard_map/attention/pallas_call | solution.py:243
  22.7 3.3 %collective-permute-start.4 = (f32[1,128]{1,0:T(1,128)S(1)}, f32[1,128]{1,0:T(1,128)S(1)}, u32[]{:S(2)}, u32[]{:S(2)}) collective-permute-start(f32[1,128]{1,0:T(1,128)S(1)} %get-tuple-element.29), channel_id=1, source_target_pairs={{0,16},{16,0},{1,17},{17,1},{2,18},{18,2},{3,19},{19,3},{4,20},{20... | collective-permute-start | bytes 1544 | tf_op jit(solution)/shard_map/ppermute | solution.py:288
  26.0 1.4 %collective-permute-start.2 = (bf16[2,128,512]{2,1,0:T(8,128)(2,1)S(1)}, bf16[2,128,512]{2,1,0:T(8,128)(2,1)S(1)}, u32[]{:S(2)}, u32[]{:S(2)}) collective-permute-start(bf16[2,128,512]{2,1,0:T(8,128)(2,1)S(1)} %get-tuple-element.27), channel_id=1, source_target_pairs={{0,15},{1,14},{2,0},{3,1},{4,2},{5,3},{6,4},{7,5},{8,6},{9,7},{10,... | collective-permute-start | bytes 786440 | tf_op jit(solution)/shard_map/ppermute | solution.py:279
  27.4 2.7 %collective-permute-start.3 = (bf16[2,128,512]{2,1,0:T(8,128)(2,1)S(1)}, bf16[2,128,512]{2,1,0:T(8,128)(2,1)S(1)}, u32[]{:S(2)}, u32[]{:S(2)}) collective-permute-start(bf16[2,128,512]{2,1,0:T(8,128)(2,1)S(1)} %get-tuple-element.28), channel_id=1, source_target_pairs={{0,15},{1,0},{2,1},{3,2},{4,3},{5,4},{6,5},{7,6},{8,7},{9,8},{10,9... | collective-permute-start | bytes 786440 | tf_op jit(solution)/shard_map/ppermute | solution.py:279
  30.1 0.0 collective-permute-done.4
  30.1 22.0 %all_to_all.8 = f32[128,1,128]{2,1,0:T(1,128)S(1)} all-to-all(f32[128,1,128]{2,1,0:T(1,128)S(1)} %broadcast_in_dim.2), channel_id=1, replica_groups=mesh['chip'=8,'core'=2,'sp'=16] {'chip','sp'}, dimensions={0} | all-to-all | bytes 131072 | tf_op jit(solution)/shard_map/all_to_all | solution.py:291
  52.1 0.0 collective-permute-done.2.one_ref
  52.1 0.0 collective-permute-done.3.two_ref
  52.1 1.0 %finish.1 = (bf16[2,128,512]{2,1,0:T(8,128)(2,1)}, f32[1,128]{1,0:T(1,128)}, f32[1,128]{1,0:T(1,128)}) custom-call(bf16[2,128,512]{2,1,0:T(8,128)(2,1)S(1)} %copy-done.1, bf16[2,128,512]{2,1,0:T(8,128)(2,1)S(1)} %get-tuple-element.26.own_ref, bf16[2,128,512]{2,1,0:T(8,128)(2,1)S(1)} %collective-permute-done.2.one_ref, ...), custom_call_target="tpu_custom_call" | custom-call | tf_op jit(solution)/shard_map/finish/pallas_call | solution.py:261
  (2 shorter events, 0.0 us)
Async XLA Ops:
  0.6 15.8 %copy-start.10 = (f32[128]{0:T(128)S(1)}, f32[128]{0:T(128)}, u32[]{:S(2)}) copy-start(f32[128]{0:T(128)} %param.13) | copy-start | bytes 1540
  0.6 15.8 %copy-start.8 = (f32[128]{0:T(128)S(1)}, f32[128]{0:T(128)}, u32[]{:S(2)}) copy-start(f32[128]{0:T(128)} %param.12) | copy-start | bytes 1540
  0.7 13.9 %collective-permute-start.1 = (bf16[2,128,512]{2,1,0:T(8,128)(2,1)}, bf16[2,128,512]{2,1,0:T(8,128)(2,1)S(1)}, u32[]{:S(2)}, u32[]{:S(2)}) collective-permute-start(bf16[2,128,512]{2,1,0:T(8,128)(2,1)} %kv_ref.1), channel_id=1, source_target_pairs={{0,2},{1,3},{2,4},{3,5},{4,6},{5,7},{6,8},{7,9},{8,10},{9,11},{10,... | collective-permute-start | bytes 786440 | tf_op jit(solution)/shard_map/ppermute | solution.py:279
  4.5 11.9 %collective-permute-start = (bf16[2,128,512]{2,1,0:T(8,128)(2,1)}, bf16[2,128,512]{2,1,0:T(8,128)(2,1)S(1)}, u32[]{:S(2)}, u32[]{:S(2)}) collective-permute-start(bf16[2,128,512]{2,1,0:T(8,128)(2,1)} %kv_ref.1), channel_id=1, source_target_pairs={{0,1},{1,2},{2,3},{3,4},{4,5},{5,6},{6,7},{7,8},{8,9},{9,10},{10,1... | collective-permute-start | bytes 786440 | tf_op jit(solution)/shard_map/ppermute | solution.py:279
  4.9 1.0 %copy-start = (bf16[2,128,512]{2,1,0:T(8,128)(2,1)S(1)}, bf16[2,128,512]{2,1,0:T(8,128)(2,1)}, u32[]{:S(2)}) copy-start(bf16[2,128,512]{2,1,0:T(8,128)(2,1)} %kv_ref.1) | copy-start | bytes 786436
  5.9 1.2 %copy-start.2 = (bf16[128,4096]{1,0:T(8,128)(2,1)S(1)}, bf16[128,4096]{1,0:T(8,128)(2,1)}, u32[]{:S(2)}) copy-start(bf16[128,4096]{1,0:T(8,128)(2,1)} %q_ref.3) | copy-start | bytes 3145732
  7.1 1.2 %copy-start.4 = (bf16[128,4096]{1,0:T(8,128)(2,1)S(1)}, bf16[128,4096]{1,0:T(8,128)(2,1)}, u32[]{:S(2)}) copy-start(bf16[128,4096]{1,0:T(8,128)(2,1)} %g_ref.3) | copy-start | bytes 3145732
  8.3 0.7 %copy-start.6 = (s32[1,1,2048]{2,1,0:T(1,128)S(1)}, s32[1,1,2048]{2,1,0:T(1,128)}, u32[]{:S(2)}) copy-start(s32[1,1,2048]{2,1,0:T(1,128)} %seg_ref.1) | copy-start | bytes 24580
  9.0 0.7 %copy-start.7 = (f32[128]{0:T(128)S(1)}, f32[128]{0:T(128)}, u32[]{:S(2)}) copy-start(f32[128]{0:T(128)} %param.12) | copy-start | bytes 1540
  9.7 0.7 %copy-start.9 = (f32[128]{0:T(128)S(1)}, f32[128]{0:T(128)}, u32[]{:S(2)}) copy-start(f32[128]{0:T(128)} %param.13) | copy-start | bytes 1540
  10.3 0.7 %copy-start.11 = (s32[1,1,16]{2,1,0:T(1,128)S(1)}, s32[1,1,16]{2,1,0:T(1,128)}, u32[]{:S(2)}) copy-start(s32[1,1,16]{2,1,0:T(1,128)} %lag_ref.1) | copy-start | bytes 196
  11.0 5.4 %copy-start.1 = (bf16[2,128,512]{2,1,0:T(8,128)(2,1)S(1)}, bf16[2,128,512]{2,1,0:T(8,128)(2,1)}, u32[]{:S(2)}) copy-start(bf16[2,128,512]{2,1,0:T(8,128)(2,1)} %kv_ref.1) | copy-start | bytes 786436
  11.0 5.4 %copy-start.3 = (bf16[128,4096]{1,0:T(8,128)(2,1)S(1)}, bf16[128,4096]{1,0:T(8,128)(2,1)}, u32[]{:S(2)}) copy-start(bf16[128,4096]{1,0:T(8,128)(2,1)} %q_ref.3) | copy-start | bytes 3145732
  11.0 5.4 %copy-start.5 = (bf16[128,4096]{1,0:T(8,128)(2,1)S(1)}, bf16[128,4096]{1,0:T(8,128)(2,1)}, u32[]{:S(2)}) copy-start(bf16[128,4096]{1,0:T(8,128)(2,1)} %g_ref.3) | copy-start | bytes 3145732
  22.7 7.4 %collective-permute-start.4 = (f32[1,128]{1,0:T(1,128)S(1)}, f32[1,128]{1,0:T(1,128)S(1)}, u32[]{:S(2)}, u32[]{:S(2)}) collective-permute-start(f32[1,128]{1,0:T(1,128)S(1)} %get-tuple-element.29), channel_id=1, source_target_pairs={{0,16},{16,0},{1,17},{17,1},{2,18},{18,2},{3,19},{19,3},{4,20},{20... | collective-permute-start | bytes 1544 | tf_op jit(solution)/shard_map/ppermute | solution.py:288
  26.0 26.1 %collective-permute-start.2 = (bf16[2,128,512]{2,1,0:T(8,128)(2,1)S(1)}, bf16[2,128,512]{2,1,0:T(8,128)(2,1)S(1)}, u32[]{:S(2)}, u32[]{:S(2)}) collective-permute-start(bf16[2,128,512]{2,1,0:T(8,128)(2,1)S(1)} %get-tuple-element.27), channel_id=1, source_target_pairs={{0,15},{1,14},{2,0},{3,1},{4,2},{5,3},{6,4},{7,5},{8,6},{9,7},{10,... | collective-permute-start | bytes 786440 | tf_op jit(solution)/shard_map/ppermute | solution.py:279
  27.4 24.7 %collective-permute-start.3 = (bf16[2,128,512]{2,1,0:T(8,128)(2,1)S(1)}, bf16[2,128,512]{2,1,0:T(8,128)(2,1)S(1)}, u32[]{:S(2)}, u32[]{:S(2)}) collective-permute-start(bf16[2,128,512]{2,1,0:T(8,128)(2,1)S(1)} %get-tuple-element.28), channel_id=1, source_target_pairs={{0,15},{1,0},{2,1},{3,2},{4,3},{5,4},{6,5},{7,6},{8,7},{9,8},{10,9... | collective-permute-start | bytes 786440 | tf_op jit(solution)/shard_map/ppermute | solution.py:279
